TPU v7x, 128 devices: a whole 4x4x4 slice. The times are simulated.
128 devices in a mesh: ctx: 16 (over y, z), head: 8 (over x, core).
Axes of the slice: x: 4, y: 4, z: 4, core: 2. Of those that a mesh axis runs over, the one named last changes fastest.
Arguments:
- query: bfloat16 [32768, 3072], P(('ctx', 'head')), may hold values from -150 to 150
- key_in: bfloat16 [32768, 3072], P(('ctx', 'head')), may hold values from -6 to 6
- value: bfloat16 [32768, 3072], P(('ctx', 'head')), may hold values from -6 to 6
- out_grad: bfloat16 [32768, 3072], P(('ctx', 'head')), may hold values from -6 to 6
- segment: int32 [32768], replicated, may hold values from 0 to 2, never falling along the last dimension, each value on 1 to 20480 neighbouring positions
- kv_list: int32 [256, 6], replicated, may hold values from 0 to 255, as said below
Outputs:
- attended: bfloat16 [32768, 3072], P(('ctx', 'head'))
- grad_query: bfloat16 [32768, 3072], P(('ctx', 'head'))
- grad_key: bfloat16 [32768, 3072], P(('ctx', 'head'))
- grad_value: bfloat16 [32768, 3072], P(('ctx', 'head'))
Inputs may be any that keep to these rules, and one draw needn't show every extreme that they name: `kv_list`: row t lists 6 different tiles and starts with t. Take the aligned ranges of 16 tiles (k*16 to k*16 + 15): every row lists exactly 3 tiles outside its own range, and the rows of one range list together exactly 2 different tiles of every other range.
All inputs are finite; a program needn't handle non-finite values.
Results may differ from a plain program's by a relative error of at most 0.04.
Values may be sent and summed in bfloat16 or wider, within the bound.
A program may use at most 192 MiB of HBM per device.

v0:
```python
import math

import jax
import jax.numpy as jnp
from jax import lax
from jax.sharding import PartitionSpec as P

HEAD_DIM = 128
TILE = 128
LIST = 6
CAP = 2


masked_score = -1e30


def request_tables(entries, n_ctx, tiles_dev):
    every_tile = jnp.arange(n_ctx * tiles_dev, dtype=jnp.int32)
    listed = jnp.any(entries[:, None] == every_tile[None, :], axis=0)
    listed = listed.reshape(n_ctx, tiles_dev).astype(jnp.int32)
    ranking = jnp.cumsum(listed, axis=1) - 1
    slot_ids = jnp.arange(CAP, dtype=jnp.int32)
    matches = (listed[:, :, None] == 1) & (ranking[:, :, None] == slot_ids[None, None, :])
    positions = jnp.arange(tiles_dev, dtype=jnp.int32)
    chosen = jnp.sum(matches.astype(jnp.int32) * positions[None, :, None], axis=1)
    filled = jnp.any(matches, axis=1).astype(jnp.int32)
    return (ranking, chosen, filled)


def body(query, key_in, value, out_grad, segment, kv_list):
    n_ctx = lax.axis_size("ctx")
    n_head = lax.axis_size("head")
    my_ctx = lax.axis_index("ctx")
    head_width = query.shape[1] // n_head
    tok_ctx = query.shape[0] * n_head
    tiles_dev = tok_ctx // TILE
    heads_dev = head_width // HEAD_DIM
    slots_all = tiles_dev + n_ctx * CAP
    my_rows = lax.dynamic_slice_in_dim(kv_list, my_ctx * tiles_dev, tiles_dev, 0)
    ranking, chosen, filled = request_tables(my_rows.reshape(-1), n_ctx, tiles_dev)

    def one_requester(entries):
        return request_tables(entries, n_ctx, tiles_dev)

    query_ctx, keys_ctx, values_ctx, grad_ctx = (
        lax.all_to_all(query, "head", split_axis=1, concat_axis=0, tiled=True),
        lax.all_to_all(key_in, "head", split_axis=1, concat_axis=0, tiled=True),
        lax.all_to_all(value, "head", split_axis=1, concat_axis=0, tiled=True),
        lax.all_to_all(out_grad, "head", split_axis=1, concat_axis=0, tiled=True),
    )
    every = jax.vmap(one_requester)(kv_list.reshape(n_ctx, tiles_dev * LIST))
    wanted = every[1][:, my_ctx]
    wanted_ok = every[2][:, my_ctx]
    key_local = keys_ctx.reshape(tiles_dev, TILE, head_width)
    value_local = values_ctx.reshape(tiles_dev, TILE, head_width)
    recv_keys = lax.all_to_all(key_local[wanted], "ctx", split_axis=0, concat_axis=0, tiled=True)
    recv_values = lax.all_to_all(
        value_local[wanted], "ctx", split_axis=0, concat_axis=0, tiled=True
    )
    recv_keys, recv_values, wanted, wanted_ok = (recv_keys, recv_values, wanted, wanted_ok)
    owner_of = my_rows // tiles_dev
    within = my_rows % tiles_dev
    slot_index = jnp.where(
        owner_of == my_ctx, within, tiles_dev + owner_of * CAP + ranking[owner_of, within]
    )
    key_source = jnp.concatenate(
        [
            keys_ctx.reshape(tiles_dev, TILE, head_width),
            recv_keys.reshape(n_ctx * CAP, TILE, head_width),
        ],
        axis=0,
    )
    value_source = jnp.concatenate(
        [
            values_ctx.reshape(tiles_dev, TILE, head_width),
            recv_values.reshape(n_ctx * CAP, TILE, head_width),
        ],
        axis=0,
    )
    seg_tiles = segment.reshape(-1, TILE)
    query_seg = lax.dynamic_slice_in_dim(seg_tiles, my_ctx * tiles_dev, tiles_dev, 0)
    key_seg = seg_tiles[my_rows].reshape(tiles_dev, LIST * TILE)
    query_tiles = query_ctx.reshape(tiles_dev, TILE, heads_dev, HEAD_DIM)
    grad_tiles = grad_ctx.reshape(tiles_dev, TILE, heads_dev, HEAD_DIM)
    group = math.gcd(tiles_dev, max(1, 512 // TILE))
    blocks = tiles_dev // group
    scale = HEAD_DIM ** (-0.5)

    def block_step(carry, block_id):
        acc_keys, acc_values = carry
        first = block_id * group
        q_block = lax.dynamic_slice_in_dim(query_tiles, first, group, 0)
        g_block = lax.dynamic_slice_in_dim(grad_tiles, first, group, 0)
        picked = lax.dynamic_slice_in_dim(slot_index, first, group, 0)
        seg_query = lax.dynamic_slice_in_dim(query_seg, first, group, 0)
        seg_keys = lax.dynamic_slice_in_dim(key_seg, first, group, 0)
        k_block = key_source[picked].reshape(group, LIST * TILE, heads_dev, HEAD_DIM)
        v_block = value_source[picked].reshape(group, LIST * TILE, heads_dev, HEAD_DIM)
        scores = (
            jnp.einsum("bqhd,bkhd->bhqk", q_block, k_block, preferred_element_type=jnp.float32)
            * scale
        )
        allowed = seg_query[:, :, None] == seg_keys[:, None, :]
        scores = jnp.where(allowed[:, None], scores, masked_score)
        top = jnp.max(scores, axis=-1, keepdims=True)
        expd = jnp.exp(scores - top)
        probs = expd / jnp.sum(expd, axis=-1, keepdims=True)
        probs_low = probs.astype(jnp.bfloat16)
        attended = jnp.einsum(
            "bhqk,bkhd->bqhd", probs_low, v_block, preferred_element_type=jnp.float32
        ).astype(jnp.bfloat16)
        grad_probs = jnp.einsum(
            "bqhd,bkhd->bhqk", g_block, v_block, preferred_element_type=jnp.float32
        )
        row_dot = jnp.sum(g_block.astype(jnp.float32) * attended.astype(jnp.float32), axis=-1)
        grad_scores = (probs * (grad_probs - jnp.transpose(row_dot, (0, 2, 1))[..., None])).astype(
            jnp.bfloat16
        )
        grad_query = (
            jnp.einsum("bhqk,bkhd->bqhd", grad_scores, k_block, preferred_element_type=jnp.float32)
            * scale
        ).astype(jnp.bfloat16)
        grad_keys = (
            jnp.einsum("bhqk,bqhd->bkhd", grad_scores, q_block, preferred_element_type=jnp.float32)
            * scale
        )
        grad_values = jnp.einsum(
            "bhqk,bqhd->bkhd", probs_low, g_block, preferred_element_type=jnp.float32
        )
        flat_slots = picked.reshape(-1)
        acc_keys = acc_keys.at[flat_slots].add(grad_keys.reshape(group * LIST, TILE * head_width))
        acc_values = acc_values.at[flat_slots].add(
            grad_values.reshape(group * LIST, TILE * head_width)
        )
        return ((acc_keys, acc_values), (attended, grad_query))

    zeros = jnp.zeros((slots_all, TILE * head_width), jnp.float32)
    (acc_keys, acc_values), (attended, grad_query) = lax.scan(
        block_step, (zeros, zeros), jnp.arange(blocks, dtype=jnp.int32)
    )
    remote_keys = acc_keys[tiles_dev:].reshape(n_ctx, CAP, TILE * head_width)
    remote_values = acc_values[tiles_dev:].reshape(n_ctx, CAP, TILE * head_width)
    back_keys, back_values = (
        lax.all_to_all(remote_keys, "ctx", split_axis=0, concat_axis=0, tiled=True),
        lax.all_to_all(remote_values, "ctx", split_axis=0, concat_axis=0, tiled=True),
    )
    keep = (wanted_ok == 1) & (jnp.arange(n_ctx, dtype=jnp.int32)[:, None] != my_ctx)
    keep_rows = keep.reshape(n_ctx * CAP, 1)
    target_rows = wanted.reshape(n_ctx * CAP)
    back_keys = jnp.where(keep_rows, back_keys.reshape(n_ctx * CAP, TILE * head_width), 0.0)
    back_values = jnp.where(keep_rows, back_values.reshape(n_ctx * CAP, TILE * head_width), 0.0)
    key_grad = acc_keys[:tiles_dev].at[target_rows].add(back_keys)
    value_grad = acc_values[:tiles_dev].at[target_rows].add(back_values)
    key_grad = key_grad.astype(jnp.bfloat16).reshape(tok_ctx, head_width)
    value_grad = value_grad.astype(jnp.bfloat16).reshape(tok_ctx, head_width)
    attended = attended.reshape(tok_ctx, head_width)
    grad_query = grad_query.reshape(tok_ctx, head_width)
    out_attended, out_query, out_key, out_value = (
        lax.all_to_all(attended, "head", split_axis=0, concat_axis=1, tiled=True),
        lax.all_to_all(grad_query, "head", split_axis=0, concat_axis=1, tiled=True),
        lax.all_to_all(key_grad, "head", split_axis=0, concat_axis=1, tiled=True),
        lax.all_to_all(value_grad, "head", split_axis=0, concat_axis=1, tiled=True),
    )
    return (out_attended, out_query, out_key, out_value)


def solution(mesh):
    in_specs = (
        P(("ctx", "head"), None),
        P(("ctx", "head"), None),
        P(("ctx", "head"), None),
        P(("ctx", "head"), None),
        P(),
        P(),
    )
    out_specs = (
        P(("ctx", "head"), None),
        P(("ctx", "head"), None),
        P(("ctx", "head"), None),
        P(("ctx", "head"), None),
    )
    return jax.shard_map(body, mesh=mesh, in_specs=in_specs, out_specs=out_specs, check_vma=False)
```

profile of v0, /device:TPU:25, one launch (start us, length us, event | category | flops | bytes accessed | tf_op | source)
XLA Modules:
  0.0 981.9 jit_solution(16831152560462871838)
XLA Ops:
  9.7 19.4 %all-to-all-done = bf16[256,8,384]{0,2,1:T(8,128)(2,1)S(1)} async-done(((bf16[256,8,384]{0,2,1:T(8,128)(2,1)}), bf16[256,8,384]{0,2,1:T(8,128)(2,1)S(1)}, u32[]{:S(2)}, u32[]{:S(2)}) %all-to-all-start) | async-done | bytes 1572896 | tf_op jit(solution)/shard_map/all_to_all | solution.py:46
  35.9 19.4 %all-to-all-done.1 = bf16[256,8,384]{2,0,1:T(8,128)(2,1)S(1)} async-done(((bf16[256,8,384]{2,0,1:T(8,128)(2,1)}), bf16[256,8,384]{2,0,1:T(8,128)(2,1)S(1)}, u32[]{:S(2)}, u32[]{:S(2)}) %all-to-all-start.1) | async-done | bytes 1572896 | tf_op jit(solution)/shard_map/all_to_all | solution.py:47
  62.2 18.1 %all-to-all-done.4 = bf16[256,8,384]{2,0,1:T(8,128)(2,1)S(1)} async-done(((bf16[256,8,384]{2,0,1:T(8,128)(2,1)}), bf16[256,8,384]{2,0,1:T(8,128)(2,1)S(1)}, u32[]{:S(2)}, u32[]{:S(2)}) %all-to-all-start.4) | async-done | bytes 1572896 | tf_op jit(solution)/shard_map/all_to_all | solution.py:48
  116.6 35.6 %all-to-all-done.5 = bf16[16,2,128,384]{3,2,1,0:T(8,128)(2,1)} async-done(((bf16[16,2,128,384]{3,2,1,0:T(8,128)(2,1)}), bf16[16,2,128,384]{3,2,1,0:T(8,128)(2,1)}, u32[]{:S(2)}, u32[]{:S(2)}) %all-to-all-start.5) | async-done | bytes 3145760 | tf_op jit(solution)/shard_map/all_to_all | solution.py:57
  152.2 8.9 all-to-all-start.2
  182.4 14.0 %all-to-all-done.2 = bf16[16,2,128,384]{3,2,1,0:T(8,128)(2,1)} async-done(((bf16[16,2,128,384]{3,2,1,0:T(8,128)(2,1)}), bf16[16,2,128,384]{3,2,1,0:T(8,128)(2,1)}, u32[]{:S(2)}, u32[]{:S(2)}) %all-to-all-start.2) | async-done | bytes 3145760 | tf_op jit(solution)/shard_map/all_to_all | solution.py:56
  209.5 477.8 %while.16 = (s32[]{:T(128)}, f32[48,49152]{1,0:T(8,128)}, f32[48,49152]{1,0:T(8,128)}, bf16[4,4,128,3,128]{2,1,0,4,3:T(4,128)(2,1)}, bf16[4,4,128,3,128]{2,1,0,4...) while((s32[]{:T(128)}, f32[48,49152]{1,0:T(8,128)}, ...), condition=%wide.region_11.12_spmd, body=%wide.region_5.11_spmd.sunk | while | flops 1829044608 | bytes 204158768 | solution.py:138
  300.0 14.6 %scatter_fusion.1 = f32[48,49152]{1,0:T(8,128)} fusion(f32[48,49152]{1,0:T(8,128)} %get-tuple-element.326, s32[24]{0:T(128)S(1)} %fusion.69, f32[24,49152]{1,0:T(8,128)} %reshape.381), kind=kCustom, calls=%fused_computation.7.clone.1 | custom fusion | flops 1179648 | bytes 14155872 | tf_op jit(solution)/shard_map/while/body/eval_jaxpr/scatter-add | solution.py:132
  314.6 14.6 %scatter_fusion = f32[48,49152]{1,0:T(8,128)} fusion(f32[48,49152]{1,0:T(8,128)} %get-tuple-element.325, s32[24]{0:T(128)S(1)} %fusion.69, f32[24,49152]{1,0:T(8,128)} %reshape.380), kind=kCustom, calls=%fused_computation.6.clone.1 | custom fusion | flops 1179648 | bytes 14155872 | tf_op jit(solution)/shard_map/while/body/eval_jaxpr/scatter-add | solution.py:131
  419.3 14.6 %scatter_fusion.1 = f32[48,49152]{1,0:T(8,128)} fusion(f32[48,49152]{1,0:T(8,128)} %get-tuple-element.326, s32[24]{0:T(128)S(1)} %fusion.69, f32[24,49152]{1,0:T(8,128)} %reshape.381), kind=kCustom, calls=%fused_computation.7.clone.1 | custom fusion | flops 1179648 | bytes 14155872 | tf_op jit(solution)/shard_map/while/body/eval_jaxpr/scatter-add | solution.py:132
  433.9 14.6 %scatter_fusion = f32[48,49152]{1,0:T(8,128)} fusion(f32[48,49152]{1,0:T(8,128)} %get-tuple-element.325, s32[24]{0:T(128)S(1)} %fusion.69, f32[24,49152]{1,0:T(8,128)} %reshape.380), kind=kCustom, calls=%fused_computation.6.clone.1 | custom fusion | flops 1179648 | bytes 14155872 | tf_op jit(solution)/shard_map/while/body/eval_jaxpr/scatter-add | solution.py:131
  538.6 14.6 %scatter_fusion.1 = f32[48,49152]{1,0:T(8,128)} fusion(f32[48,49152]{1,0:T(8,128)} %get-tuple-element.326, s32[24]{0:T(128)S(1)} %fusion.69, f32[24,49152]{1,0:T(8,128)} %reshape.381), kind=kCustom, calls=%fused_computation.7.clone.1 | custom fusion | flops 1179648 | bytes 14155872 | tf_op jit(solution)/shard_map/while/body/eval_jaxpr/scatter-add | solution.py:132
  553.2 14.6 %scatter_fusion = f32[48,49152]{1,0:T(8,128)} fusion(f32[48,49152]{1,0:T(8,128)} %get-tuple-element.325, s32[24]{0:T(128)S(1)} %fusion.69, f32[24,49152]{1,0:T(8,128)} %reshape.380), kind=kCustom, calls=%fused_computation.6.clone.1 | custom fusion | flops 1179648 | bytes 14155872 | tf_op jit(solution)/shard_map/while/body/eval_jaxpr/scatter-add | solution.py:131
  658.0 14.6 %scatter_fusion.1 = f32[48,49152]{1,0:T(8,128)} fusion(f32[48,49152]{1,0:T(8,128)} %get-tuple-element.326, s32[24]{0:T(128)S(1)} %fusion.69, f32[24,49152]{1,0:T(8,128)} %reshape.381), kind=kCustom, calls=%fused_computation.7.clone.1 | custom fusion | flops 1179648 | bytes 14155872 | tf_op jit(solution)/shard_map/while/body/eval_jaxpr/scatter-add | solution.py:132
  672.6 14.6 %scatter_fusion = f32[48,49152]{1,0:T(8,128)} fusion(f32[48,49152]{1,0:T(8,128)} %get-tuple-element.325, s32[24]{0:T(128)S(1)} %fusion.69, f32[24,49152]{1,0:T(8,128)} %reshape.380), kind=kCustom, calls=%fused_computation.6.clone.1 | custom fusion | flops 1179648 | bytes 14155872 | tf_op jit(solution)/shard_map/while/body/eval_jaxpr/scatter-add | solution.py:131
  700.6 8.1 all-to-all-start.8
  722.2 55.0 %all-to-all-done.8 = f32[16,2,49152]{2,1,0:T(2,128)} async-done(((f32[16,2,49152]{2,1,0:T(2,128)}), f32[16,2,49152]{2,1,0:T(2,128)}, u32[]{:S(2)}, u32[]{:S(2)}) %all-to-all-start.8) | async-done | bytes 6291488 | tf_op jit(solution)/shard_map/all_to_all | solution.py:144
  777.2 13.0 %all-to-all-start.10 = ((f32[16,2,49152]{2,1,0:T(2,128)}), f32[16,2,49152]{2,1,0:T(2,128)}, u32[]{:S(2)}, u32[]{:S(2)}) async-start(f32[16,2,49152]{2,1,0:T(2,128)} %reshape.245), calls=%async_computation.10 | async-start | bytes 12582912 | tf_op jit(solution)/shard_map/all_to_all | solution.py:145
  792.8 66.1 %all-to-all-done.10 = f32[16,2,49152]{2,1,0:T(2,128)} async-done(((f32[16,2,49152]{2,1,0:T(2,128)}), f32[16,2,49152]{2,1,0:T(2,128)}, u32[]{:S(2)}, u32[]{:S(2)}) %all-to-all-start.10) | async-done | bytes 6291488 | tf_op jit(solution)/shard_map/all_to_all | solution.py:145
  858.8 13.5 %all-to-all-start.7 = ((bf16[8,256,384]{1,2,0:T(8,128)(2,1)}), bf16[8,256,384]{1,2,0:T(8,128)(2,1)}, u32[]{:S(2)}, u32[]{:S(2)}) async-start(bf16[8,256,384]{1,2,0:T(8,128)(2,1)} %copy.172), calls=%async_computation.7 | async-start | bytes 3145728 | tf_op jit(solution)/shard_map/all_to_all | solution.py:160
  903.3 10.1 %broadcast_select_fusion = (f32[32,49152]{1,0:T(8,128)}, f32[32,49152]{1,0:T(8,128)}) fusion(f32[32,49152]{1,0:T(8,128)} %reshape.246, pred[32]{0:T(512)(128)(4,1)S(1)} %and.39, f32[32,49152]{1,0:T(8,128)} %reshape.244), kind=kLoop, calls=%fused_computation.44 | loop fusion | flops 3145728 | bytes 25165856 | tf_op jit(solution)/shard_map/jit(_where)/select_n | solution.py:151
  913.4 10.8 %scatter_fusion.2 = f32[16,49152]{1,0:T(8,128)S(1)} fusion(f32[16,49152]{1,0:T(8,128)S(1)} %slice.12, s32[32]{0:T(128)S(1)} %fusion.24, f32[32,49152]{1,0:T(8,128)} %get-tuple-element.211), kind=kCustom, calls=%fused_computation.8 | custom fusion | flops 1572864 | bytes 18874496 | tf_op jit(solution)/shard_map/scatter-add | solution.py:152
  935.1 10.8 %scatter_fusion.3 = f32[16,49152]{1,0:T(8,128)S(1)} fusion(f32[16,49152]{1,0:T(8,128)S(1)} %slice.14, s32[32]{0:T(128)S(1)} %fusion.24, f32[32,49152]{1,0:T(8,128)} %get-tuple-element.210), kind=kCustom, calls=%fused_computation.9 | custom fusion | flops 1572864 | bytes 18874496 | tf_op jit(solution)/shard_map/scatter-add | solution.py:153
  966.8 12.1 %all-to-all-done.11 = bf16[8,256,384]{2,1,0:T(8,128)(2,1)S(1)} async-done(((bf16[8,256,384]{2,1,0:T(8,128)(2,1)}), bf16[8,256,384]{2,1,0:T(8,128)(2,1)S(1)}, u32[]{:S(2)}, u32[]{:S(2)}) %all-to-all-start.11) | async-done | bytes 1572896 | tf_op jit(solution)/shard_map/all_to_all | solution.py:162
  (308 shorter events, 545.2 us)
Async XLA Ops:
  0.6 162.5 %copy-start = (s32[32768]{0:T(1024)S(1)}, s32[32768]{0:T(1024)}, u32[]{:S(2)}) copy-start(s32[32768]{0:T(1024)} %param.12) | copy-start | bytes 393220
  0.6 7.7 copy-start.11
  3.4 25.7 %all-to-all-start = ((bf16[256,8,384]{0,2,1:T(8,128)(2,1)}), bf16[256,8,384]{0,2,1:T(8,128)(2,1)S(1)}, u32[]{:S(2)}, u32[]{:S(2)}) async-start(bf16[256,8,384]{0,2,1:T(8,128)(2,1)} %bitcast.9), calls=%async_computation | async-start | bytes 3145728 | tf_op jit(solution)/shard_map/all_to_all | solution.py:46
  9.7 24.9 %copy-start.12 = (bf16[256,3072]{1,0:T(8,128)(2,1)S(1)}, bf16[256,3072]{1,0:T(8,128)(2,1)}, u32[]{:S(2)}) copy-start(bf16[256,3072]{1,0:T(8,128)(2,1)} %param.10) | copy-start | bytes 4718596
  30.2 25.1 %all-to-all-start.1 = ((bf16[256,8,384]{2,0,1:T(8,128)(2,1)}), bf16[256,8,384]{2,0,1:T(8,128)(2,1)S(1)}, u32[]{:S(2)}, u32[]{:S(2)}) async-start(bf16[256,8,384]{2,0,1:T(8,128)(2,1)} %bitcast.78), calls=%async_computation.1 | async-start | bytes 3145728 | tf_op jit(solution)/shard_map/all_to_all | solution.py:47
  55.3 25.1 %all-to-all-start.4 = ((bf16[256,8,384]{2,0,1:T(8,128)(2,1)}), bf16[256,8,384]{2,0,1:T(8,128)(2,1)S(1)}, u32[]{:S(2)}, u32[]{:S(2)}) async-start(bf16[256,8,384]{2,0,1:T(8,128)(2,1)} %bitcast.130), calls=%async_computation.4 | async-start | bytes 3145728 | tf_op jit(solution)/shard_map/all_to_all | solution.py:48
  59.6 25.8 %copy-start.19 = (s32[256,6]{0,1:T(8,128)S(1)}, s32[256,6]{0,1:T(8,128)}, u32[]{:S(2)}) copy-start(s32[256,6]{0,1:T(8,128)} %param.13) | copy-start | bytes 18436
  80.4 25.9 %all-to-all-start.3 = ((bf16[256,8,384]{0,2,1:T(8,128)(2,1)}), bf16[256,8,384]{0,2,1:T(8,128)(2,1)}, u32[]{:S(2)}, u32[]{:S(2)}) async-start(bf16[256,8,384]{0,2,1:T(8,128)(2,1)} %bitcast.129), calls=%async_computation.3 | async-start | bytes 3145728 | tf_op jit(solution)/shard_map/all_to_all | solution.py:49
  106.2 45.9 %all-to-all-start.5 = ((bf16[16,2,128,384]{3,2,1,0:T(8,128)(2,1)}), bf16[16,2,128,384]{3,2,1,0:T(8,128)(2,1)}, u32[]{:S(2)}, u32[]{:S(2)}) async-start(bf16[16,2,128,384]{3,2,1,0:T(8,128)(2,1)} %bitcast.127), calls=%async_computation.5 | async-start | bytes 6291456 | tf_op jit(solution)/shard_map/all_to_all | solution.py:57
  152.2 44.3 %all-to-all-start.2 = ((bf16[16,2,128,384]{3,2,1,0:T(8,128)(2,1)}), bf16[16,2,128,384]{3,2,1,0:T(8,128)(2,1)}, u32[]{:S(2)}, u32[]{:S(2)}) async-start(bf16[16,2,128,384]{3,2,1,0:T(8,128)(2,1)} %bitcast.126), calls=%async_computation.2 | async-start | bytes 6291456 | tf_op jit(solution)/shard_map/all_to_all | solution.py:56
  291.3 7.3 copy-start.9
  410.6 7.3 copy-start.9
  530.0 7.3 copy-start.9
  700.6 76.6 %all-to-all-start.8 = ((f32[16,2,49152]{2,1,0:T(2,128)}), f32[16,2,49152]{2,1,0:T(2,128)}, u32[]{:S(2)}, u32[]{:S(2)}) async-start(f32[16,2,49152]{2,1,0:T(2,128)} %reshape.243), calls=%async_computation.8 | async-start | bytes 12582912 | tf_op jit(solution)/shard_map/all_to_all | solution.py:144
  722.2 68.0 %copy-start.13 = (bf16[4,4,128,3,128]{2,1,0,4,3:T(4,128)(2,1)S(1)}, bf16[4,4,128,3,128]{2,1,0,4,3:T(4,128)(2,1)}, u32[]{:S(2)}) copy-start(bf16[4,4,128,3,128]{2,1,0,4,3:T(4,128)(2,1)} %get-tuple-element.75) | copy-start | bytes 4718596
  777.2 81.6 %all-to-all-start.10 = ((f32[16,2,49152]{2,1,0:T(2,128)}), f32[16,2,49152]{2,1,0:T(2,128)}, u32[]{:S(2)}, u32[]{:S(2)}) async-start(f32[16,2,49152]{2,1,0:T(2,128)} %reshape.245), calls=%async_computation.10 | async-start | bytes 12582912 | tf_op jit(solution)/shard_map/all_to_all | solution.py:145
  791.3 81.3 %copy-start.15 = (s32[16,16,16]{2,1,0:T(8,128)S(1)}, s32[16,16,16]{2,1,0:T(8,128)}, u32[]{:S(2)}) copy-start(s32[16,16,16]{2,1,0:T(8,128)} %copy-done.14) | copy-start | bytes 49156
  791.3 81.3 %copy-start.17 = (pred[16,16,16]{2,1,0:T(8,128)(4,1)S(1)}, pred[16,16,16]{2,1,0:T(8,128)(4,1)}, u32[]{:S(2)}) copy-start(pred[16,16,16]{2,1,0:T(8,128)(4,1)} %copy-done.16) | copy-start | bytes 12292
  791.3 82.5 %copy-start.18 = (s32[16,2]{1,0:T(8,128)S(1)}, s32[16,2]{1,0:T(8,128)}, u32[]{:S(2)}) copy-start(s32[16,2]{1,0:T(8,128)} %get-tuple-element.200) | copy-start | bytes 388
  858.8 39.6 %all-to-all-start.7 = ((bf16[8,256,384]{1,2,0:T(8,128)(2,1)}), bf16[8,256,384]{1,2,0:T(8,128)(2,1)}, u32[]{:S(2)}, u32[]{:S(2)}) async-start(bf16[8,256,384]{1,2,0:T(8,128)(2,1)} %copy.172), calls=%async_computation.7 | async-start | bytes 3145728 | tf_op jit(solution)/shard_map/all_to_all | solution.py:160
  898.5 29.8 %all-to-all-start.6 = ((bf16[8,256,384]{1,2,0:T(8,128)(2,1)}), bf16[8,256,384]{1,2,0:T(8,128)(2,1)}, u32[]{:S(2)}, u32[]{:S(2)}) async-start(bf16[8,256,384]{1,2,0:T(8,128)(2,1)} %copy.170), calls=%async_computation.6 | async-start | bytes 3145728 | tf_op jit(solution)/shard_map/all_to_all | solution.py:159
  928.2 25.6 %all-to-all-start.9 = ((bf16[8,256,384]{2,1,0:T(8,128)(2,1)}), bf16[8,256,384]{2,1,0:T(8,128)(2,1)}, u32[]{:S(2)}, u32[]{:S(2)}) async-start(bf16[8,256,384]{2,1,0:T(8,128)(2,1)} %all_to_all.139), calls=%async_computation.9 | async-start | bytes 3145728 | tf_op jit(solution)/shard_map/all_to_all | solution.py:161
  953.9 25.1 %all-to-all-start.11 = ((bf16[8,256,384]{2,1,0:T(8,128)(2,1)}), bf16[8,256,384]{2,1,0:T(8,128)(2,1)S(1)}, u32[]{:S(2)}, u32[]{:S(2)}) async-start(bf16[8,256,384]{2,1,0:T(8,128)(2,1)} %all_to_all.144), calls=%async_computation.11 | async-start | bytes 3145728 | tf_op jit(solution)/shard_map/all_to_all | solution.py:162
  965.1 16.4 %copy-start.1 = (s32[32768]{0:T(1024)S(1)}, s32[32768]{0:T(1024)}, u32[]{:S(2)}) copy-start(s32[32768]{0:T(1024)} %param.12) | copy-start | bytes 393220
  (32 other events, 104.2 us)
where the time goes:
time: 999 us; the launch traced here: 982 us
  local copies, waits for them, and re-layouts  387 us (39%)
  waiting for transfers between devices  250 us (25%)
  other arithmetic  186 us (19%)
  starting transfers between devices  83.8 us (8%)
  matrix products  70.4 us (7%)
    all_to_all x1, waiting for transfers between devices, body(): lax.all_to_all(remote_values, 'ctx', split_axis=0, concat_axis=0, tiled=T...  66.1 us
    scatter-add x4, other arithmetic, block_step(): acc_values.at[flat_slots]  58.4 us
    scatter-add x4, other arithmetic, block_step(): acc_keys.at[flat_slots]  58.3 us
    all_to_all x1, waiting for transfers between devices, body(): lax.all_to_all(remote_keys, 'ctx', split_axis=0, concat_axis=0, tiled=True)  55 us
    reshape x8, local copies, waits for them, and re-layouts, block_step(): value_source[picked].reshape(group, LIST * TILE, heads_dev, HEAD_DIM)  37.1 us
    reshape x8, local copies, waits for them, and re-layouts, block_step(): key_source[picked].reshape(group, LIST * TILE, heads_dev, HEAD_DIM)  37 us
    all_to_all x1, waiting for transfers between devices, body(): lax.all_to_all(value_local[wanted], 'ctx', split_axis=0, concat_axis=0, t...  35.6 us
    reshape x4, local copies, waits for them, and re-layouts, block_step(): grad_values.reshape(group * LIST, TILE * head_width)  29.2 us
  transfers between devices with their start and end apart: 12, of which 10 were waited for; matrix products, arithmetic and copies ran while one was open for 13% of the time, Pallas kernels for 0%

commit v1 on v0

v1 whole, which is shorter than its diff:
```python
import functools

import jax
import jax.numpy as jnp
from jax import lax
from jax.experimental import pallas as pl
from jax.experimental.pallas import tpu as pltpu
from jax.sharding import PartitionSpec as P

HEAD_DIM = 128
TILE = 128
LIST = 6
CAP = 2
TPD = 16
NCTX = 16
NHEAD = 8
HPD = 3
NREM = (NCTX - 1) * CAP
SLOTS = TPD + NREM
ROWS = TPD * LIST
HALF = ROWS // 2
MASKED = -1e30
SCALE = HEAD_DIM**-0.5
LOG2E = 1.4426950408889634
MESH = pl.DeviceIdType.MESH

OFFSETS = (
    (0, 1), (0, 3), (1, 0), (3, 0), (0, 2), (2, 0), (1, 1), (3, 3),
    (1, 3), (3, 1), (1, 2), (3, 2), (2, 1), (2, 3), (2, 2),
)

T_SLOT = 0
T_TILE = T_SLOT + ROWS
T_WANT = T_TILE + ROWS
T_LPERM = T_WANT + NREM
T_LSAME = T_LPERM + HALF
T_LLAST = T_LSAME + HALF
T_RPERM = T_LLAST + TPD
T_RSAME = T_RPERM + HALF
T_RLAST = T_RSAME + HALF
T_BPERM = T_RLAST + NREM
T_BSAME = T_BPERM + NREM
T_BLAST = T_BSAME + NREM
T_EDGE = T_BLAST + TPD
T_SIZE = T_EDGE + 2


def relative(y, z, other):
    return ((other // 4 - y) % 4) * 4 + (other % 4 - z) % 4


def sorted_runs(keys, valid, count):
    n = keys.shape[0]
    index = jnp.arange(n, dtype=jnp.int32)
    full = jnp.where(valid, keys * n + index, 1 << 20)
    place = jnp.sum((full[None, :] < full[:, None]).astype(jnp.int32), axis=1)
    places = jnp.arange(count, dtype=jnp.int32)
    hit = (place[None, :] == places[:, None]) & valid[None, :]
    perm = jnp.sum(jnp.where(hit, index[None, :], 0), axis=1)
    key_at = jnp.sum(jnp.where(hit, keys[None, :], 0), axis=1)
    before = jnp.concatenate([jnp.full((1,), -1, jnp.int32), key_at[:-1]])
    return perm, (key_at == before).astype(jnp.int32)


def tables(segment, kv_list):
    me = lax.axis_index("ctx")
    y, z = me // 4, me % 4
    entries = kv_list.reshape(NCTX, ROWS)
    owner, within = entries // TPD, entries % TPD
    mine = lax.dynamic_index_in_dim(entries, me, 0, keepdims=False)
    own, inside = mine // TPD, mine % TPD
    same_owner = own[None, :] == own[:, None]
    low = jnp.min(jnp.where(same_owner, inside[None, :], TPD), axis=1)
    rank = (inside != low).astype(jnp.int32)
    local = own == me
    slot = jnp.where(local, inside, TPD + CAP * (relative(y, z, own) - 1) + rank)
    step = jnp.arange(1, NCTX, dtype=jnp.int32)
    requester = ((y + step // 4) % 4) * 4 + (z + step % 4) % 4
    asked = owner == me
    first = jnp.min(jnp.where(asked, within, TPD), axis=1)
    second = jnp.max(jnp.where(asked, within, -1), axis=1)
    pick = requester[:, None] == jnp.arange(NCTX, dtype=jnp.int32)[None, :]
    want = jnp.stack(
        [
            jnp.sum(jnp.where(pick, first[None, :], 0), axis=1),
            jnp.sum(jnp.where(pick, second[None, :], 0), axis=1),
        ],
        axis=1,
    ).reshape(NREM)
    tiles = jnp.arange(TPD, dtype=jnp.int32)
    rems = jnp.arange(NREM, dtype=jnp.int32)
    l_perm, l_same = sorted_runs(slot, local, HALF)
    l_last = jnp.sum((local[None, :] & (slot[None, :] <= tiles[:, None])).astype(jnp.int32), axis=1) - 1
    r_perm, r_same = sorted_runs(slot, ~local, HALF)
    r_last = jnp.sum((~local[None, :] & (slot[None, :] - TPD <= rems[:, None])).astype(jnp.int32), axis=1) - 1
    b_perm, b_same = sorted_runs(want, jnp.ones((NREM,), bool), NREM)
    upto = jnp.sum((want[None, :] <= tiles[:, None]).astype(jnp.int32), axis=1)
    b_last = jnp.where(jnp.any(want[None, :] == tiles[:, None], axis=1), upto, 0)
    edges = jnp.stack([jnp.sum((segment < 1).astype(jnp.int32)), jnp.sum((segment < 2).astype(jnp.int32))])
    return jnp.concatenate(
        [slot, mine, want, l_perm, l_same, l_last, r_perm, r_same, r_last, b_perm, b_same, b_last, edges]
    ).astype(jnp.int32)


def dot_nt(a, b):
    return lax.dot_general(a, b, (((1,), (1,)), ((), ())), preferred_element_type=jnp.float32)


def dot_nn(a, b):
    return lax.dot_general(a, b, (((1,), (0,)), ((), ())), preferred_element_type=jnp.float32)


def dot_tn(a, b):
    return lax.dot_general(a, b, (((0,), (0,)), ((), ())), preferred_element_type=jnp.float32)


def attend(tab, me, q, g, k_all, v_all, o_out, dq_out, c_key, c_value):
    edge1, edge2 = tab[T_EDGE], tab[T_EDGE + 1]
    end = NCTX * TPD * TILE

    def one(i, carry):
        query, grad = q[i], g[i]
        slots = [tab[T_SLOT + i * LIST + j] for j in range(LIST)]
        keys = jnp.concatenate([k_all[s] for s in slots], axis=0)
        values = jnp.concatenate([v_all[s] for s in slots], axis=0)
        scores = dot_nt(query, keys) * (SCALE * LOG2E)
        at = (me * TPD + i) * TILE + lax.broadcasted_iota(jnp.int32, (TILE, TILE), 0)
        start = jnp.where(at >= edge2, edge2, jnp.where(at >= edge1, edge1, 0))
        stop = jnp.where(at >= edge2, end, jnp.where(at >= edge1, edge2, edge1))
        lane = lax.broadcasted_iota(jnp.int32, (TILE, TILE), 1)
        parts = []
        for j in range(LIST):
            key_at = tab[T_TILE + i * LIST + j] * TILE + lane
            allowed = (key_at >= start) & (key_at < stop)
            parts.append(jnp.where(allowed, scores[:, j * TILE : (j + 1) * TILE], MASKED))
        scores = jnp.concatenate(parts, axis=1)
        top = jnp.max(scores, axis=1, keepdims=True)
        expd = jnp.exp2(scores - top)
        probs = expd * (1.0 / jnp.sum(expd, axis=1, keepdims=True))
        low = probs.astype(jnp.bfloat16)
        attended = dot_nn(low, values).astype(jnp.bfloat16)
        o_out[i] = attended
        grad_probs = dot_nt(grad, values)
        row_dot = jnp.sum(grad.astype(jnp.float32) * attended.astype(jnp.float32), axis=1, keepdims=True)
        grad_scores = (probs * (grad_probs - row_dot)).astype(jnp.bfloat16)
        dq_out[i] = (dot_nn(grad_scores, keys) * SCALE).astype(jnp.bfloat16)
        key_part = (dot_tn(grad_scores, query) * SCALE).astype(jnp.bfloat16)
        value_part = dot_tn(low, grad).astype(jnp.bfloat16)
        c_key[pl.ds(i * LIST, LIST)] = key_part.reshape(LIST, TILE, HEAD_DIM)
        c_value[pl.ds(i * LIST, LIST)] = value_part.reshape(LIST, TILE, HEAD_DIM)
        return carry

    lax.fori_loop(0, TPD, one, 0)


def run_sums(tab, perm, same, count, parts, out, shift=0):
    def one(p, total):
        total = jnp.where(tab[same + p] == 1, total, 0.0) + parts[tab[perm + p]].astype(jnp.float32)
        out[p + shift] = total.astype(out.dtype)
        return total

    lax.fori_loop(0, count, one, jnp.zeros((TILE, HEAD_DIM), jnp.float32))


def wait_bytes(ref, sem):
    pltpu.make_async_copy(ref, ref, sem).wait()


def kernel(tab, q_in, k_in, v_in, g_in, o_out, dq_out, dk_out, dv_out, *scratch):
    it = iter(scratch)

    def take(n):
        return [next(it) for _ in range(n)]

    q_loc, g_loc, k_loc, v_loc = take(HPD), take(HPD), take(HPD), take(HPD)
    k_all, v_all = take(HPD), take(HPD)
    k_stage, v_stage = take(HPD), take(HPD)
    k_back, v_back = take(HPD), take(HPD)
    o_stage, dq_stage, dk_stage, dv_stage = take(HPD), take(HPD), take(HPD), take(HPD)
    k_sum, v_sum = take(HPD), take(HPD)
    c_key, c_value, run_local, run_remote, run_back = take(5)
    x_send, x_recv, c_send, c_recv, b_send, b_recv, y_send, y_recv = take(8)

    me, head = lax.axis_index("ctx"), lax.axis_index("head")
    y, z = me // 4, me % 4

    barrier = pltpu.get_barrier_semaphore()
    for d in range(1, NHEAD):
        pl.semaphore_signal(barrier, inc=1, device_id=(me, (head + d) % NHEAD), device_id_type=MESH)
    for dy, dz in OFFSETS:
        peer = ((y + dy) % 4) * 4 + (z + dz) % 4
        pl.semaphore_signal(barrier, inc=1, device_id=(peer, head), device_id_type=MESH)
    pl.semaphore_wait(barrier, NHEAD - 1 + NCTX - 1)

    def columns(owner, h):
        return pl.ds(pl.multiple_of((owner * HPD + h) * HEAD_DIM, HEAD_DIM), HEAD_DIM)

    def pair(index):
        return pl.ds(2 * index, 2)

    def send_in(a, h):
        src, dst = (q_in, k_in, v_in, g_in)[a], (q_loc, k_loc, v_loc, g_loc)[a][h]
        for d in range(1, NHEAD):
            peer = (head + d) % NHEAD
            pltpu.make_async_remote_copy(
                src_ref=src.at[:, :, columns(peer, h)],
                dst_ref=dst.at[pair(head)],
                send_sem=x_send.at[a],
                recv_sem=x_recv.at[a, h],
                device_id=(me, peer),
                device_id_type=MESH,
            ).start()
        pltpu.make_async_copy(src.at[:, :, columns(head, h)], dst.at[pair(head)], x_recv.at[a, h]).start()

    def wait_in(a, h):
        wait_bytes((q_loc, k_loc, v_loc, g_loc)[a][h], x_recv.at[a, h])

    def send_out(a, h):
        src, dst = (o_stage, dq_stage, dk_stage, dv_stage)[a][h], (o_out, dq_out, dk_out, dv_out)[a]
        for d in range(1, NHEAD):
            peer = (head + d) % NHEAD
            pltpu.make_async_remote_copy(
                src_ref=src.at[pair(peer)],
                dst_ref=dst.at[:, :, columns(head, h)],
                send_sem=y_send.at[a],
                recv_sem=y_recv.at[a],
                device_id=(me, peer),
                device_id_type=MESH,
            ).start()
        pltpu.make_async_copy(src.at[pair(head)], dst.at[:, :, columns(head, h)], y_recv.at[a]).start()

    def send_ctx(stage, landing, base, send_sem, recv_sem):
        for dy, dz in OFFSETS:
            there = dy * 4 + dz - 1
            here = ((-dy) % 4) * 4 + (-dz) % 4 - 1
            peer = ((y + dy) % 4) * 4 + (z + dz) % 4
            pltpu.make_async_remote_copy(
                src_ref=stage.at[pl.ds(CAP * there, CAP)],
                dst_ref=landing.at[pl.ds(base + CAP * here, CAP)],
                send_sem=send_sem,
                recv_sem=recv_sem,
                device_id=(peer, head),
                device_id_type=MESH,
            ).start()

    Q, K, V, G = 0, 1, 2, 3
    for a, h in ((K, 0), (V, 0), (K, 1), (V, 1), (Q, 0), (G, 0), (K, 2), (V, 2), (Q, 1), (G, 1), (Q, 2), (G, 2)):
        send_in(a, h)

    def forward_tiles(a, h):
        wait_in(a, h)
        s = a - K
        local, stage, everything = (k_loc, v_loc)[s][h], (k_stage, v_stage)[s][h], (k_all, v_all)[s][h]

        def pack(p, carry):
            stage[p] = local[tab[T_WANT + p]]
            return carry

        lax.fori_loop(0, NREM, pack, 0)
        send_ctx(stage, everything, TPD, c_send.at[s, h], c_recv.at[s, h])

        def keep(p, carry):
            everything[p] = local[p]
            return carry

        lax.fori_loop(0, TPD, keep, 0)

    for h in range(HPD):
        forward_tiles(K, h)
        forward_tiles(V, h)

    for h in range(HPD):
        wait_in(Q, h)
        wait_in(G, h)
        for s in range(2):
            wait_bytes((k_all, v_all)[s][h].at[pl.ds(TPD, NREM)], c_recv.at[s, h])
        attend(tab, me, q_loc[h], g_loc[h], k_all[h], v_all[h], o_stage[h], dq_stage[h], c_key, c_value)
        send_out(0, h)
        send_out(1, h)
        for s in range(2):
            parts, stage, landing = (c_key, c_value)[s], (k_stage, v_stage)[s][h], (k_back, v_back)[s][h]
            run_sums(tab, T_RPERM, T_RSAME, HALF, parts, run_remote)
            wait_bytes(stage, c_send.at[s, h])

            def fill(p, carry, stage=stage):
                stage[p] = run_remote[tab[T_RLAST + p]]
                return carry

            lax.fori_loop(0, NREM, fill, 0)
            send_ctx(stage, landing, 0, b_send.at[s, h], b_recv.at[s, h])
        for s in range(2):
            parts, sums = (c_key, c_value)[s], (k_sum, v_sum)[s][h]
            run_sums(tab, T_LPERM, T_LSAME, HALF, parts, run_local)

            def settle(p, carry, sums=sums):
                sums[p] = run_local[tab[T_LLAST + p]]
                return carry

            lax.fori_loop(0, TPD, settle, 0)

    run_back[0] = jnp.zeros((TILE, HEAD_DIM), jnp.float32)
    for h in range(HPD):
        for s in range(2):
            back, sums, stage = (k_back, v_back)[s][h], (k_sum, v_sum)[s][h], (dk_stage, dv_stage)[s][h]
            wait_bytes(back, b_recv.at[s, h])
            run_sums(tab, T_BPERM, T_BSAME, NREM, back, run_back, shift=1)

            def finish(p, carry, sums=sums, stage=stage):
                stage[p] = (sums[p] + run_back[tab[T_BLAST + p]]).astype(jnp.bfloat16)
                return carry

            lax.fori_loop(0, TPD, finish, 0)
            send_out(2 + s, h)

    sent = CAP * (NHEAD - 1) * HPD
    for a in range(4):
        wait_bytes(k_all[0].at[pl.ds(0, sent)], x_send.at[a])
        wait_bytes(k_all[0].at[pl.ds(0, sent)], y_send.at[a])
        wait_bytes((o_out, dq_out, dk_out, dv_out)[a], y_recv.at[a])
    for s in range(2):
        for h in range(HPD):
            wait_bytes((k_stage, v_stage)[s][h], b_send.at[s, h])


def body(query, key_in, value, out_grad, segment, kv_list):
    tab = tables(segment, kv_list)
    tokens, width = query.shape
    shape = (tokens // TILE, TILE, width)
    bf16, f32 = jnp.bfloat16, jnp.float32

    def vmem(n, dtype=bf16):
        return pltpu.VMEM((n, TILE, HEAD_DIM), dtype)

    scratch = (
        [vmem(TPD)] * (4 * HPD)
        + [vmem(SLOTS)] * (2 * HPD)
        + [vmem(NREM)] * (2 * HPD)
        + [vmem(NREM)] * (2 * HPD)
        + [vmem(TPD)] * (4 * HPD)
        + [vmem(TPD, f32)] * (2 * HPD)
        + [vmem(ROWS), vmem(ROWS), vmem(HALF, f32), vmem(HALF), vmem(NREM + 1, f32)]
        + [
            pltpu.SemaphoreType.DMA((4,)),
            pltpu.SemaphoreType.DMA((4, HPD)),
            pltpu.SemaphoreType.DMA((2, HPD)),
            pltpu.SemaphoreType.DMA((2, HPD)),
            pltpu.SemaphoreType.DMA((2, HPD)),
            pltpu.SemaphoreType.DMA((2, HPD)),
            pltpu.SemaphoreType.DMA((4,)),
            pltpu.SemaphoreType.DMA((4,)),
        ]
    )
    outs = pl.pallas_call(
        kernel,
        out_shape=[jax.ShapeDtypeStruct(shape, bf16)] * 4,
        in_specs=[pl.BlockSpec(memory_space=pltpu.SMEM)] + [pl.BlockSpec(memory_space=pl.ANY)] * 4,
        out_specs=[pl.BlockSpec(memory_space=pl.ANY)] * 4,
        scratch_shapes=scratch,
        compiler_params=pltpu.CompilerParams(
            collective_id=0, has_side_effects=True, vmem_limit_bytes=60 * 1024 * 1024
        ),
        cost_estimate=pl.CostEstimate(flops=7_250_000_000, bytes_accessed=12_600_000, transcendentals=4_718_592),
        name="sparse_attention",
    )(tab, *(a.reshape(shape) for a in (query, key_in, value, out_grad)))
    return tuple(o.reshape(tokens, width) for o in outs)


def solution(mesh):
    tokens = P(("ctx", "head"), None)
    return jax.shard_map(
        body,
        mesh=mesh,
        in_specs=(tokens, tokens, tokens, tokens, P(), P()),
        out_specs=(tokens, tokens, tokens, tokens),
        check_vma=False,
    )
```

time: 999 us -> 195 us (0.20); the launches traced: 982 us -> 195 us
  local copies, waits for them, and re-layouts: 387 us -> 11.1 us
  waiting for transfers between devices: 250 us -> 0 us
  other arithmetic: 186 us -> 4.37 us
  Pallas kernels: 0 us -> 178 us
  starting transfers between devices: 83.8 us -> 0 us
  matrix products: 70.4 us -> 0 us
    all_to_all x12 -> x0, waiting for transfers between devices: 250 us -> none  [the longest x1 66.1 us: body(): lax.all_to_all(remote_values, 'ctx', split_axis=0, concat_axis=0, tiled=T...]
    pallas_call x0 -> x1, Pallas kernels: none -> 178 us  [body(): pl.pallas_call(kernel, out_shape=[jax.ShapeDtypeStruct(shape, bf16)] * 4,...]
    reshape x35 -> x2, local copies, waits for them, and re-layouts: 171 us -> 0.2 us  [the longest x1 0.11 us: tables(): entries = kv_list.reshape(NCTX, ROWS)]
    scatter-add x10 -> x0, other arithmetic: 138 us -> none  [the longest x4 58.4 us: block_step(): acc_values.at[flat_slots]]
    all_to_all x12 -> x0, starting transfers between devices: 83.8 us -> none  [the longest x1 13.5 us: body(): lax.all_to_all(grad_query, 'head', split_axis=0, concat_axis=1, tiled=True)]
    dot_general x20 -> x0, matrix products: 46.6 us -> none  [the longest x4 18.6 us: block_step(): jnp.einsum('bhqk,bqhd->bkhd', grad_scores, q_block, preferred_element_typ...]
    gather x13 -> x0, local copies, waits for them, and re-layouts: 45 us -> none  [the longest x4 18.9 us: block_step(): key_source[picked].reshape(group, LIST * TILE, heads_dev, HEAD_DIM)]
    mul x4 -> x0, local copies, waits for them, and re-layouts: 28.2 us -> none  [block_step(): jnp.einsum('bhqk,bqhd->bkhd', grad_scores, q_block, preferred_element_typ...]
  transfers between devices with their start and end apart: 12 -> 0, of which waited for: 10 -> 0; matrix products, arithmetic and copies ran while one was open for 13% -> 0% of each run, Pallas kernels for 0% -> 0%
where the time goes in v1:
time: 195 us
  Pallas kernels  178 us (91%)
  local copies, waits for them, and re-layouts  11.1 us (6%)
  other arithmetic  4.37 us (2%)
    pallas_call x1, Pallas kernels, body(): pl.pallas_call(kernel, out_shape=[jax.ShapeDtypeStruct(shape, bf16)] * 4,...  178 us
    unnamed x11, local copies, waits for them, and re-layouts  8.7 us

profile of v1, /device:TPU:25, one launch (start us, length us, event | category | flops | bytes accessed | tf_op | source)
XLA Modules:
  0.0 194.7 jit_solution(2231297544001281954)
XLA Ops:
  0.7 1.6 convert_reduce_fusion
  2.2 0.7 select_reduce_fusion.10
  3.1 0.1 reduce_min.30
  3.3 0.1 reduce_max.18
  3.4 0.2 select_reduce_fusion.9
  3.8 0.1 convert_reduce_fusion.6
  3.9 0.1 fusion.6
  4.0 0.2 convert_reduce_fusion.4
  4.2 0.1 select_reduce_fusion.5
  4.4 0.8 copy.14
  5.2 0.1 reshape.273
  5.4 0.2 select_reduce_fusion
  5.7 0.1 convert_reduce_fusion.5
  5.8 0.1 convert_reduce_fusion.7
  5.9 0.2 convert_reduce_fusion.2
  6.1 0.2 select_reduce_fusion.1
  6.4 2.0 %concatenate.15.tab = s32[538]{0:T(1024)} concatenate(s32[96]{0:T(128)S(1)} %get-tuple-element.30, s32[96]{0:T(128)S(1)} %bitcast.43, s32[30]{0:T(128)S(1)} %reshape.274, s32[48]{0:T(128)S(1)} %get-tuple-element.22, s32[48]{0:T(128)S(1)} %compare_convert_fusion.2, s32[16]{0:T(128)S(1)} %get-tuple-element.40, s32[48]{0:T(128)S(1)} %get-tuple-element.17, ...), dimensions={0} | concatenate | bytes 4304 | tf_op jit(solution)/shard_map/concatenate | solution.py:100
  8.4 178.4 %sparse_attention.1 = (bf16[2,128,3072]{2,1,0:T(8,128)(2,1)}, bf16[2,128,3072]{2,1,0:T(8,128)(2,1)}, bf16[2,128,3072]{2,1,0:T(8,128)(2,1)}, bf16[2,128,3072]{2,1,0:T(8,128)(2,1)}) custom-call(s32[538]{0:T(1024)} %concatenate.15.tab, bf16[2,128,3072]{2,1,0:T(8,128)(2,1)} %bitcast.54, bf16[2,128,3072]{2,1,0:T(8,128)(2,1)} %bitcast.55, ...), custom_call_target="tpu_custom_call" | custom-call | flops 7249999872 | bytes 12600000 | tf_op jit(solution)/shard_map/sparse_attention/pallas_call | solution.py:353
  186.8 2.8 %copy.20 = bf16[256,3072]{1,0:T(8,128)(2,1)} copy(bf16[256,3072]{1,0:T(8,128)(2,1)} %bitcast.42) | data formatting | bytes 3145728
  189.6 1.1 copy.21
  190.7 0.8 copy-done.1
  191.6 1.1 copy.22
  192.7 0.8 copy-done
  193.5 1.1 copy.23
  (23 shorter events, 0.7 us)
Async XLA Ops:
  186.8 2.8 %copy-start.2 = (bf16[2,128,3072]{2,1,0:T(8,128)(2,1)S(1)}, bf16[2,128,3072]{2,1,0:T(8,128)(2,1)}, u32[]{:S(2)}) copy-start(bf16[2,128,3072]{2,1,0:T(8,128)(2,1)} %get-tuple-element.9) | copy-start | bytes 4718596
  189.6 2.0 %copy-start.1 = (bf16[2,128,3072]{2,1,0:T(8,128)(2,1)S(1)}, bf16[2,128,3072]{2,1,0:T(8,128)(2,1)}, u32[]{:S(2)}) copy-start(bf16[2,128,3072]{2,1,0:T(8,128)(2,1)} %get-tuple-element.10) | copy-start | bytes 4718596
  191.6 2.0 %copy-start = (bf16[2,128,3072]{2,1,0:T(8,128)(2,1)S(1)}, bf16[2,128,3072]{2,1,0:T(8,128)(2,1)}, u32[]{:S(2)}) copy-start(bf16[2,128,3072]{2,1,0:T(8,128)(2,1)} %get-tuple-element.11) | copy-start | bytes 4718596

commit v2 on v1

v2 whole, which is shorter than its diff:
```python
import jax
import jax.numpy as jnp
from jax import lax
from jax.experimental import pallas as pl
from jax.experimental.pallas import tpu as pltpu
from jax.sharding import PartitionSpec as P

HEAD_DIM = 128
TILE = 128
LIST = 6
CAP = 2
TPD = 16
NCTX = 16
NHEAD = 8
HPD = 3
NREM = (NCTX - 1) * CAP
SLOTS = TPD + NREM
ROWS = TPD * LIST
HALF = ROWS // 2
MASKED = -1e30
SCALE = HEAD_DIM**-0.5
LOG2E = 1.4426950408889634
MESH = pl.DeviceIdType.MESH

OFFSETS = (
    (0, 1), (2, 3), (0, 3), (2, 1), (1, 0), (3, 2), (3, 0), (1, 2),
    (0, 2), (2, 0), (2, 2), (1, 1), (3, 3), (1, 3), (3, 1),
)

WHOLE = ((0, TILE),)
HALVES = ((0, TILE // 2), (TILE // 2, TILE // 2))
PARTS_IN = {(s, h): WHOLE for s in range(2) for h in range(HPD)} | {(0, 0): HALVES}
PARTS_BACK = {(s, h): WHOLE for s in range(2) for h in range(HPD)} | {(1, HPD - 1): HALVES}
MOST_PARTS = 2

T_SLOT, T_TILE, T_WANT = 0, 1, 2
T_LPERM, T_LSAME, T_LLAST = 3, 4, 5
T_RPERM, T_RSAME, T_RLAST = 6, 7, 8
T_BPERM, T_BSAME, T_BLAST = 9, 10, 11
T_EDGE = 12
T_ROWS = 16


def relative(y, z, other):
    return (((other >> 2) - y) & 3) * 4 + (((other & 3) - z) & 3)


def build_tables(me, kv, seg, table):
    y, z = me // 4, me % 4
    big = 1 << 20
    sub = lax.broadcasted_iota(jnp.int32, (TILE, TILE), 0)
    lane = lax.broadcasted_iota(jnp.int32, (TILE, TILE), 1)
    at = lax.broadcasted_iota(jnp.int32, (TILE, 1), 0)
    eye = sub == lane

    def to_row(col):
        return jnp.sum(jnp.where(eye, col, 0), axis=0, keepdims=True)

    def count(mask):
        return jnp.sum(jnp.where(mask, 1, 0), axis=0, keepdims=True)

    def runs(key_c, key_r, valid_c, valid_r):
        full_c = jnp.where(valid_c, key_c * TILE + at, big)
        full_r = jnp.where(valid_r, key_r * TILE + lane, big)
        place = jnp.sum(jnp.where(full_r < full_c, 1, 0), axis=1, keepdims=True)
        hit = (place == lane) & valid_c
        after = (place + 1 == lane) & valid_c
        perm = jnp.sum(jnp.where(hit, sub, 0), axis=0, keepdims=True)
        key = jnp.sum(jnp.where(hit, key_c + 1, 0), axis=0, keepdims=True)
        before = jnp.sum(jnp.where(after, key_c + 1, 0), axis=0, keepdims=True)
        return perm, jnp.where(key == before, 1, 0)

    wide = lax.broadcasted_iota(jnp.int32, (TILE, NCTX * TPD), 1)
    rows = [kv[j : j + 1, :] for j in range(LIST)]
    low = jnp.full((1, NCTX * TPD), TPD, jnp.int32)
    high = jnp.full((1, NCTX * TPD), -1, jnp.int32)
    for row in rows:
        asked = (row >> 4) == me
        low = jnp.where(asked, jnp.minimum(low, row & 15), low)
        high = jnp.where(asked, jnp.maximum(high, row & 15), high)
    step = (at >> 1) + 1
    asker = ((y + (step >> 2)) & 3) * 4 + ((z + (step & 3)) & 3)
    group = (wide >> 4) == asker
    first = jnp.min(jnp.where(group, low, TPD), axis=1, keepdims=True)
    second = jnp.max(jnp.where(group, high, -1), axis=1, keepdims=True)
    want_c = jnp.clip(jnp.where((at & 1) == 0, first, second), 0, TPD - 1)
    want_r = to_row(want_c)
    mine_c = jnp.zeros((TILE, 1), jnp.int32)
    for j in range(LIST):
        here = (wide == me * TPD + (at & 15)) & ((at >> 4) == j)
        mine_c = mine_c + jnp.sum(jnp.where(here, rows[j], 0), axis=1, keepdims=True)
    mine_r = to_row(mine_c)
    own_c, own_r = mine_c >> 4, mine_r >> 4
    in_c, in_r = mine_c & 15, mine_r & 15
    real_c, real_r = at < ROWS, lane < ROWS
    lowest = jnp.min(jnp.where((own_c == own_r) & real_r, in_r, TPD), axis=1, keepdims=True)
    rank = jnp.where(in_c != lowest, 1, 0)
    slot_c = jnp.where(own_c == me, in_c, TPD + CAP * (relative(y, z, own_c) - 1) + rank)
    slot_r = to_row(slot_c)
    local_c, local_r = (own_c == me) & real_c, (own_r == me) & real_r
    other_c, other_r = (own_c != me) & real_c, (own_r != me) & real_r
    l_perm, l_same = runs(slot_c, slot_r, local_c, local_r)
    r_perm, r_same = runs(slot_c, slot_r, other_c, other_r)
    asked_c, asked_r = at < NREM, lane < NREM
    b_perm, b_same = runs(want_c, want_r, asked_c, asked_r)
    upto = count((want_c <= lane) & asked_c)
    b_last = jnp.where(count((want_c == lane) & asked_c) > 0, upto, 0)
    edges = []
    for value in (1, 2):
        per_lane = jnp.sum(jnp.where(seg[...] < value, 1, 0), axis=0, keepdims=True)
        edges.append(jnp.sum(per_lane, axis=1, keepdims=True))
    lane_r = lax.broadcasted_iota(jnp.int32, (1, TILE), 1)
    found = {
        T_SLOT: slot_r,
        T_TILE: mine_r,
        T_WANT: want_r,
        T_LPERM: l_perm,
        T_LSAME: l_same,
        T_LLAST: jnp.clip(count((slot_c <= lane) & local_c) - 1, 0, HALF - 1),
        T_RPERM: r_perm,
        T_RSAME: r_same,
        T_RLAST: jnp.clip(count((slot_c - TPD <= lane) & other_c) - 1, 0, HALF - 1),
        T_BPERM: b_perm,
        T_BSAME: b_same,
        T_BLAST: b_last,
        T_EDGE: jnp.where(lane_r == 0, edges[0], edges[1]),
    }
    none = jnp.zeros((1, TILE), jnp.int32)
    table[...] = jnp.concatenate([found.get(r, none) for r in range(T_ROWS)], axis=0)


def dot_nt(a, b):
    return lax.dot_general(a, b, (((1,), (1,)), ((), ())), preferred_element_type=jnp.float32)


def dot_nn(a, b):
    return lax.dot_general(a, b, (((1,), (0,)), ((), ())), preferred_element_type=jnp.float32)


def dot_tn(a, b):
    return lax.dot_general(a, b, (((0,), (0,)), ((), ())), preferred_element_type=jnp.float32)


def attend(tab, me, q, g, k_all, v_all, o_out, dq_out, c_key, c_value):
    edge1, edge2 = tab[T_EDGE, 0], tab[T_EDGE, 1]
    end = NCTX * TPD * TILE

    def one(i, carry):
        query, grad = q[i], g[i]
        slots = [tab[T_SLOT, j * TPD + i] for j in range(LIST)]
        keys = jnp.concatenate([k_all[s] for s in slots], axis=0)
        values = jnp.concatenate([v_all[s] for s in slots], axis=0)
        scores = dot_nt(query, keys) * (SCALE * LOG2E)
        at = (me * TPD + i) * TILE + lax.broadcasted_iota(jnp.int32, (TILE, TILE), 0)
        start = jnp.where(at >= edge2, edge2, jnp.where(at >= edge1, edge1, 0))
        stop = jnp.where(at >= edge2, end, jnp.where(at >= edge1, edge2, edge1))
        lane = lax.broadcasted_iota(jnp.int32, (TILE, TILE), 1)
        parts = []
        for j in range(LIST):
            key_at = tab[T_TILE, j * TPD + i] * TILE + lane
            allowed = (key_at >= start) & (key_at < stop)
            parts.append(jnp.where(allowed, scores[:, j * TILE : (j + 1) * TILE], MASKED))
        scores = jnp.concatenate(parts, axis=1)
        top = jnp.max(scores, axis=1, keepdims=True)
        expd = jnp.exp2(scores - top)
        probs = expd * (1.0 / jnp.sum(expd, axis=1, keepdims=True))
        low = probs.astype(jnp.bfloat16)
        attended = dot_nn(low, values).astype(jnp.bfloat16)
        o_out[i] = attended
        grad_probs = dot_nt(grad, values)
        row_dot = jnp.sum(grad.astype(jnp.float32) * attended.astype(jnp.float32), axis=1, keepdims=True)
        grad_scores = (probs * (grad_probs - row_dot)).astype(jnp.bfloat16)
        dq_out[i] = (dot_nn(grad_scores, keys) * SCALE).astype(jnp.bfloat16)
        key_part = (dot_tn(grad_scores, query) * SCALE).astype(jnp.bfloat16)
        value_part = dot_tn(low, grad).astype(jnp.bfloat16)
        for j in range(LIST):
            c_key[j * TPD + i] = key_part[j * TILE : (j + 1) * TILE]
            c_value[j * TPD + i] = value_part[j * TILE : (j + 1) * TILE]
        return carry

    lax.fori_loop(0, TPD, one, 0)


def run_sums(tab, perm, same, count, parts, out, shift=0, rows=TILE):
    def one(p, total):
        total = jnp.where(tab[same, p] == 1, total, 0.0) + parts[tab[perm, p]].astype(jnp.float32)
        out[p + shift, pl.ds(0, rows)] = total.astype(out.dtype)
        return total

    lax.fori_loop(0, count, one, jnp.zeros((rows, HEAD_DIM), jnp.float32))


def wait_bytes(ref, sem):
    pltpu.make_async_copy(ref, ref, sem).wait()


def kernel(q_in, k_in, v_in, g_in, seg_in, kv_in, o_out, dq_out, dk_out, dv_out, *scratch):
    it = iter(scratch)

    def take(n):
        return [next(it) for _ in range(n)]

    def take_parts(parts):
        return {(s, h): take(len(parts[s, h])) for s in range(2) for h in range(HPD)}

    q_loc, g_loc = take(HPD), take(HPD)
    kv_loc, kv_back = take_parts(PARTS_IN), take_parts(PARTS_BACK)
    k_all, v_all = take(HPD), take(HPD)
    k_stage, v_stage = take(HPD), take(HPD)
    o_stage, dq_stage, dk_stage, dv_stage = take(HPD), take(HPD), take(HPD), take(HPD)
    k_sum, v_sum = take(HPD), take(HPD)
    c_key, c_value, run_local, run_remote, run_back = take(5)
    kv, seg, table, tab, t_sem = take(5)
    x_send, x_recv, c_send, c_recv, b_send, b_recv, y_send, y_recv = take(8)

    me, head = lax.axis_index("ctx"), lax.axis_index("head")
    y, z = me // 4, me % 4

    fetches = [pltpu.make_async_copy(kv_in, kv, t_sem.at[0]), pltpu.make_async_copy(seg_in, seg, t_sem.at[1])]
    for fetch in fetches:
        fetch.start()

    barrier = pltpu.get_barrier_semaphore()
    for d in range(1, NHEAD):
        pl.semaphore_signal(barrier, inc=1, device_id=(me, (head + d) % NHEAD), device_id_type=MESH)
    for dy, dz in OFFSETS:
        peer = ((y + dy) % 4) * 4 + (z + dz) % 4
        pl.semaphore_signal(barrier, inc=1, device_id=(peer, head), device_id_type=MESH)
    pl.semaphore_wait(barrier, NHEAD - 1 + NCTX - 1)

    def columns(owner, h):
        return pl.ds(pl.multiple_of((owner * HPD + h) * HEAD_DIM, HEAD_DIM), HEAD_DIM)

    def pair(index):
        return pl.ds(2 * index, 2)

    def send_in(src, dst, rows, h, send_sem, recv_sem):
        for d in range(1, NHEAD):
            peer = (head + d) % NHEAD
            pltpu.make_async_remote_copy(
                src_ref=src.at[:, pl.ds(*rows), columns(peer, h)],
                dst_ref=dst.at[pair(head)],
                send_sem=send_sem,
                recv_sem=recv_sem,
                device_id=(me, peer),
                device_id_type=MESH,
            ).start()
        pltpu.make_async_copy(src.at[:, pl.ds(*rows), columns(head, h)], dst.at[pair(head)], recv_sem).start()

    def send_kv(s, h):
        for n, rows in enumerate(PARTS_IN[s, h]):
            send_in((k_in, v_in)[s], kv_loc[s, h][n], rows, h, x_send.at[2 + s], x_recv.at[2 + s, h, n])

    def send_qg(h):
        send_in(q_in, q_loc[h], WHOLE[0], h, x_send.at[0], x_recv.at[0, h, 0])
        send_in(g_in, g_loc[h], WHOLE[0], h, x_send.at[1], x_recv.at[1, h, 0])

    def send_out(a, h, rows):
        src, dst = (o_stage, dq_stage, dk_stage, dv_stage)[a][h], (o_out, dq_out, dk_out, dv_out)[a]
        for d in range(1, NHEAD):
            peer = (head + d) % NHEAD
            pltpu.make_async_remote_copy(
                src_ref=src.at[pair(peer), pl.ds(*rows)],
                dst_ref=dst.at[:, pl.ds(*rows), columns(head, h)],
                send_sem=y_send.at[a],
                recv_sem=y_recv.at[a],
                device_id=(me, peer),
                device_id_type=MESH,
            ).start()
        pltpu.make_async_copy(
            src.at[pair(head), pl.ds(*rows)], dst.at[:, pl.ds(*rows), columns(head, h)], y_recv.at[a]
        ).start()

    def send_ctx(stage, landing, base, rows, landing_rows, send_sem, recv_sem):
        for dy, dz in OFFSETS:
            there = dy * 4 + dz - 1
            here = ((-dy) % 4) * 4 + (-dz) % 4 - 1
            peer = ((y + dy) % 4) * 4 + (z + dz) % 4
            pltpu.make_async_remote_copy(
                src_ref=stage.at[pl.ds(CAP * there, CAP), pl.ds(*rows)],
                dst_ref=landing.at[pl.ds(base + CAP * here, CAP), pl.ds(*landing_rows)],
                send_sem=send_sem,
                recv_sem=recv_sem,
                device_id=(peer, head),
                device_id_type=MESH,
            ).start()

    def forward_tiles(s, h):
        stage, everything = (k_stage, v_stage)[s][h], (k_all, v_all)[s][h]
        for n, rows in enumerate(PARTS_IN[s, h]):
            local = kv_loc[s, h][n]
            wait_bytes(local, x_recv.at[2 + s, h, n])

            def pack(p, carry, local=local, rows=rows):
                stage[p, pl.ds(*rows)] = local[tab[T_WANT, p]]
                return carry

            lax.fori_loop(0, NREM, pack, 0)
            send_ctx(stage, everything, TPD, rows, rows, c_send.at[s, h, n], c_recv.at[s, h, n])

            def keep(p, carry, local=local, rows=rows):
                everything[p, pl.ds(*rows)] = local[p]
                return carry

            lax.fori_loop(0, TPD, keep, 0)

    send_kv(0, 0)
    send_kv(1, 0)
    for fetch in fetches:
        fetch.wait()
    build_tables(me, kv, seg, table)
    to_scalar = pltpu.make_async_copy(table, tab, t_sem.at[2])
    to_scalar.start()
    to_scalar.wait()
    send_kv(0, 1)
    forward_tiles(0, 0)
    send_kv(1, 1)
    send_qg(0)
    forward_tiles(1, 0)
    send_kv(0, 2)
    send_kv(1, 2)
    forward_tiles(0, 1)
    send_qg(1)
    forward_tiles(1, 1)
    send_qg(2)
    forward_tiles(0, 2)
    forward_tiles(1, 2)

    for h in range(HPD):
        wait_bytes(q_loc[h], x_recv.at[0, h, 0])
        wait_bytes(g_loc[h], x_recv.at[1, h, 0])
        for s in range(2):
            for n, rows in enumerate(PARTS_IN[s, h]):
                wait_bytes((k_all, v_all)[s][h].at[pl.ds(TPD, NREM), pl.ds(*rows)], c_recv.at[s, h, n])
        attend(tab, me, q_loc[h], g_loc[h], k_all[h], v_all[h], o_stage[h], dq_stage[h], c_key, c_value)
        send_out(0, h, WHOLE[0])
        send_out(1, h, WHOLE[0])
        for s in range(2):
            stage = (k_stage, v_stage)[s][h]
            run_sums(tab, T_RPERM, T_RSAME, HALF, (c_key, c_value)[s], run_remote)
            for n, rows in enumerate(PARTS_IN[s, h]):
                wait_bytes(stage.at[:, pl.ds(*rows)], c_send.at[s, h, n])

            def fill(p, carry, stage=stage):
                stage[p] = run_remote[tab[T_RLAST, p]]
                return carry

            lax.fori_loop(0, NREM, fill, 0)
            for n, rows in enumerate(PARTS_BACK[s, h]):
                landing = kv_back[s, h][n]
                send_ctx(stage, landing, 0, rows, (0, rows[1]), b_send.at[s, h, n], b_recv.at[s, h, n])
        for s in range(2):
            sums = (k_sum, v_sum)[s][h]
            run_sums(tab, T_LPERM, T_LSAME, HALF, (c_key, c_value)[s], run_local)

            def settle(p, carry, sums=sums):
                sums[p] = run_local[tab[T_LLAST, p]]
                return carry

            lax.fori_loop(0, TPD, settle, 0)

    run_back[0] = jnp.zeros((TILE, HEAD_DIM), jnp.float32)
    for h in range(HPD):
        for s in range(2):
            sums, stage = (k_sum, v_sum)[s][h], (dk_stage, dv_stage)[s][h]
            for n, rows in enumerate(PARTS_BACK[s, h]):
                back = kv_back[s, h][n]
                wait_bytes(back, b_recv.at[s, h, n])
                run_sums(tab, T_BPERM, T_BSAME, NREM, back, run_back, shift=1, rows=rows[1])

                def finish(p, carry, sums=sums, stage=stage, rows=rows):
                    total = sums[p, pl.ds(*rows)] + run_back[tab[T_BLAST, p], pl.ds(0, rows[1])]
                    stage[p, pl.ds(*rows)] = total.astype(jnp.bfloat16)
                    return carry

                lax.fori_loop(0, TPD, finish, 0)
                send_out(2 + s, h, rows)

    sent = CAP * (NHEAD - 1) * HPD
    for a in range(4):
        wait_bytes(k_all[0].at[pl.ds(0, sent)], x_send.at[a])
        wait_bytes(k_all[0].at[pl.ds(0, sent)], y_send.at[a])
        wait_bytes((o_out, dq_out, dk_out, dv_out)[a], y_recv.at[a])
    for s in range(2):
        for h in range(HPD):
            for n, rows in enumerate(PARTS_BACK[s, h]):
                wait_bytes((k_stage, v_stage)[s][h].at[:, pl.ds(*rows)], b_send.at[s, h, n])


def hand_over(*refs):
    source, result, (held, come, go) = refs[:4], refs[4:8], refs[8:]
    pieces = [(a, p) for a in range(4) for p in range(2)]
    coming = [pltpu.make_async_copy(source[a].at[p], held.at[a, p], come.at[a, p]) for a, p in pieces]
    going = [pltpu.make_async_copy(held.at[a, p], result[a].at[p], go.at[a, p]) for a, p in pieces]
    for copy in coming:
        copy.start()
    for copy, onward in zip(coming, going):
        copy.wait()
        onward.start()
    for onward in going:
        onward.wait()


def body(query, key_in, value, out_grad, segment, kv_list):
    tokens, width = query.shape
    shape = (tokens // TILE, TILE, width)
    bf16, f32 = jnp.bfloat16, jnp.float32

    def vmem(n, dtype=bf16, rows=TILE):
        return pltpu.VMEM((n, rows, HEAD_DIM), dtype)

    def vmem_parts(n, parts):
        return [vmem(n, rows=rows) for s in range(2) for h in range(HPD) for _, rows in parts[s, h]]

    scratch = (
        [vmem(TPD)] * (2 * HPD)
        + vmem_parts(TPD, PARTS_IN)
        + vmem_parts(NREM, PARTS_BACK)
        + [vmem(SLOTS)] * (2 * HPD)
        + [vmem(NREM)] * (2 * HPD)
        + [vmem(TPD)] * (4 * HPD)
        + [vmem(TPD, f32)] * (2 * HPD)
        + [vmem(ROWS), vmem(ROWS), vmem(HALF, f32), vmem(HALF), vmem(NREM + 1, f32)]
        + [
            pltpu.VMEM((LIST, NCTX * TPD), jnp.int32),
            pltpu.VMEM((NCTX * TPD, TILE), jnp.int32),
            pltpu.VMEM((T_ROWS, TILE), jnp.int32),
            pltpu.SMEM((T_ROWS, TILE), jnp.int32),
            pltpu.SemaphoreType.DMA((3,)),
            pltpu.SemaphoreType.DMA((4,)),
            pltpu.SemaphoreType.DMA((4, HPD, MOST_PARTS)),
            pltpu.SemaphoreType.DMA((2, HPD, MOST_PARTS)),
            pltpu.SemaphoreType.DMA((2, HPD, MOST_PARTS)),
            pltpu.SemaphoreType.DMA((2, HPD, MOST_PARTS)),
            pltpu.SemaphoreType.DMA((2, HPD, MOST_PARTS)),
            pltpu.SemaphoreType.DMA((4,)),
            pltpu.SemaphoreType.DMA((4,)),
        ]
    )
    outs = pl.pallas_call(
        kernel,
        out_shape=[jax.ShapeDtypeStruct(shape, bf16)] * 4,
        in_specs=[pl.BlockSpec(memory_space=pl.ANY)] * 6,
        out_specs=[pl.BlockSpec(memory_space=pl.ANY)] * 4,
        scratch_shapes=scratch,
        compiler_params=pltpu.CompilerParams(
            collective_id=0, has_side_effects=True, vmem_limit_bytes=60 * 1024 * 1024
        ),
        cost_estimate=pl.CostEstimate(flops=7_250_000_000, bytes_accessed=12_600_000, transcendentals=4_718_592),
        name="sparse_attention",
    )(*(a.reshape(shape) for a in (query, key_in, value, out_grad)), segment.reshape(NCTX * TPD, TILE), kv_list.T)
    outs = pl.pallas_call(
        hand_over,
        out_shape=[jax.ShapeDtypeStruct(shape, bf16)] * 4,
        in_specs=[pl.BlockSpec(memory_space=pl.ANY)] * 4,
        out_specs=[pl.BlockSpec(memory_space=pl.ANY)] * 4,
        scratch_shapes=[
            pltpu.VMEM((4,) + shape, bf16),
            pltpu.SemaphoreType.DMA((4, 2)),
            pltpu.SemaphoreType.DMA((4, 2)),
        ],
        compiler_params=pltpu.CompilerParams(vmem_limit_bytes=60 * 1024 * 1024),
        name="hand_over",
    )(*outs)
    return tuple(o.reshape(tokens, width) for o in outs)


def solution(mesh):
    tokens = P(("ctx", "head"), None)
    return jax.shard_map(
        body,
        mesh=mesh,
        in_specs=(tokens, tokens, tokens, tokens, P(), P()),
        out_specs=(tokens, tokens, tokens, tokens),
        check_vma=False,
    )
```

time: 195 us -> 173 us (0.89)
  local copies, waits for them, and re-layouts: 11.1 us -> 0 us
  Pallas kernels: 178 us -> 170 us
  other arithmetic: 4.37 us -> 0 us
    pallas_call x1, Pallas kernels: 178 us -> 165 us  [body(): pl.pallas_call(kernel, out_shape=[jax.ShapeDtypeStruct(shape, bf16)] * 4,...]
    unnamed x11 -> x0, local copies, waits for them, and re-layouts: 8.7 us -> none
    pallas_call x0 -> x1, Pallas kernels: none -> 5.51 us  [body(): pl.pallas_call(hand_over, out_shape=[jax.ShapeDtypeStruct(shape, bf16)] *...]
    reduce_sum x9 -> x0, other arithmetic: 2.73 us -> none  [the longest x1 1.58 us: tables(): jnp.sum((segment < 2).astype(jnp.int32))]
    concatenate x1 -> x0, local copies, waits for them, and re-layouts: 1.98 us -> none  [tables(): jnp.concatenate([slot, mine, want, l_perm, l_same, l_last, r_perm, r_same...]
where the time goes in v2:
time: 173 us; the launch traced here: 171 us
  Pallas kernels  170 us (98%)
    pallas_call x1, Pallas kernels, body(): pl.pallas_call(kernel, out_shape=[jax.ShapeDtypeStruct(shape, bf16)] * 4,...  165 us
    pallas_call x1, Pallas kernels, body(): pl.pallas_call(hand_over, out_shape=[jax.ShapeDtypeStruct(shape, bf16)] *...  5.51 us

profile of v2, /device:TPU:25, one launch (start us, length us, event | category | flops | bytes accessed | tf_op | source)
XLA Modules:
  0.0 170.9 jit_solution(11668896568448378316)
XLA Ops:
  0.6 164.7 %sparse_attention.1 = (bf16[2,128,3072]{2,1,0:T(8,128)(2,1)}, bf16[2,128,3072]{2,1,0:T(8,128)(2,1)}, bf16[2,128,3072]{2,1,0:T(8,128)(2,1)}, bf16[2,128,3072]{2,1,0:T(8,128)(2,1)}) custom-call(bf16[2,128,3072]{2,1,0:T(8,128)(2,1)} %bitcast.10, bf16[2,128,3072]{2,1,0:T(8,128)(2,1)} %bitcast.11, bf16[2,128,3072]{2,1,0:T(8,128)(2,1)} %bitcast.12, ...), custom_call_target="tpu_custom_call" | custom-call | flops 7249999872 | bytes 12600000 | tf_op jit(solution)/shard_map/sparse_attention/pallas_call | solution.py:440
  165.4 5.5 %hand_over.1 = (bf16[2,128,3072]{2,1,0:T(8,128)(2,1)}, bf16[2,128,3072]{2,1,0:T(8,128)(2,1)}, bf16[2,128,3072]{2,1,0:T(8,128)(2,1)}, bf16[2,128,3072]{2,1,0:T(8,128)(2,1)}) custom-call(bf16[2,128,3072]{2,1,0:T(8,128)(2,1)} %get-tuple-element.12.refs_0_, bf16[2,128,3072]{2,1,0:T(8,128)(2,1)} %get-tuple-element.13.refs_1_, ...), custom_call_target="tpu_custom_call" | custom-call | tf_op jit(solution)/shard_map/hand_over/pallas_call | solution.py:452

commit v3 on v2

--- a/solution.py
+++ b/solution.py
@@ -28,12 +28,14 @@
 )
 
 WHOLE = ((0, TILE),)
-HALVES = ((0, TILE // 2), (TILE // 2, TILE // 2))
-PARTS_IN = {(s, h): WHOLE for s in range(2) for h in range(HPD)} | {(0, 0): HALVES}
-PARTS_BACK = {(s, h): WHOLE for s in range(2) for h in range(HPD)} | {(1, HPD - 1): HALVES}
-MOST_PARTS = 2
-
-T_SLOT, T_TILE, T_WANT = 0, 1, 2
+RISING = ((0, 32), (32, 32), (64, 64))
+FALLING = ((0, 64), (64, 32), (96, 32))
+PARTS_IN = {(s, h): WHOLE for s in range(2) for h in range(HPD)} | {(0, 0): RISING}
+PARTS_BACK = {(s, h): WHOLE for s in range(2) for h in range(HPD)} | {(1, HPD - 1): FALLING}
+MOST_PARTS = 3
+LATE = {(1, 1, 0): ((1, 2, 0),), (0, 2, 0): ((1, 2, 1), (1, 2, 2))}
+
+T_SLOT, T_TILE = 0, 1
 T_LPERM, T_LSAME, T_LLAST = 3, 4, 5
 T_RPERM, T_RSAME, T_RLAST = 6, 7, 8
 T_BPERM, T_BSAME, T_BLAST = 9, 10, 11
@@ -45,16 +47,36 @@
     return (((other >> 2) - y) & 3) * 4 + (((other & 3) - z) & 3)
 
 
-def build_tables(me, kv, seg, table):
+def wanted_tiles(me, kv):
+    y, z = me // 4, me % 4
+    at = lax.broadcasted_iota(jnp.int32, (TILE, 1), 0)
+    wide = lax.broadcasted_iota(jnp.int32, (TILE, NCTX * TPD), 1)
+    low = jnp.full((1, NCTX * TPD), TPD, jnp.int32)
+    high = jnp.full((1, NCTX * TPD), -1, jnp.int32)
+    for j in range(LIST):
+        row = kv[j : j + 1, :]
+        asked = (row >> 4) == me
+        low = jnp.where(asked, jnp.minimum(low, row & 15), low)
+        high = jnp.where(asked, jnp.maximum(high, row & 15), high)
+    step = (at >> 1) + 1
+    asker = ((y + (step >> 2)) & 3) * 4 + ((z + (step & 3)) & 3)
+    group = (wide >> 4) == asker
+    first = jnp.min(jnp.where(group, low, TPD), axis=1, keepdims=True)
+    second = jnp.max(jnp.where(group, high, -1), axis=1, keepdims=True)
+    return jnp.clip(jnp.where((at & 1) == 0, first, second), 0, TPD - 1)
+
+
+def diagonal(col):
+    eye = lax.broadcasted_iota(jnp.int32, (TILE, TILE), 0) == lax.broadcasted_iota(jnp.int32, (TILE, TILE), 1)
+    return jnp.sum(jnp.where(eye, col, 0), axis=0, keepdims=True)
+
+
+def build_tables(me, kv, seg, want_r, table):
     y, z = me // 4, me % 4
     big = 1 << 20
     sub = lax.broadcasted_iota(jnp.int32, (TILE, TILE), 0)
     lane = lax.broadcasted_iota(jnp.int32, (TILE, TILE), 1)
     at = lax.broadcasted_iota(jnp.int32, (TILE, 1), 0)
-    eye = sub == lane
-
-    def to_row(col):
-        return jnp.sum(jnp.where(eye, col, 0), axis=0, keepdims=True)
 
     def count(mask):
         return jnp.sum(jnp.where(mask, 1, 0), axis=0, keepdims=True)
@@ -72,31 +94,19 @@
 
     wide = lax.broadcasted_iota(jnp.int32, (TILE, NCTX * TPD), 1)
     rows = [kv[j : j + 1, :] for j in range(LIST)]
-    low = jnp.full((1, NCTX * TPD), TPD, jnp.int32)
-    high = jnp.full((1, NCTX * TPD), -1, jnp.int32)
-    for row in rows:
-        asked = (row >> 4) == me
-        low = jnp.where(asked, jnp.minimum(low, row & 15), low)
-        high = jnp.where(asked, jnp.maximum(high, row & 15), high)
-    step = (at >> 1) + 1
-    asker = ((y + (step >> 2)) & 3) * 4 + ((z + (step & 3)) & 3)
-    group = (wide >> 4) == asker
-    first = jnp.min(jnp.where(group, low, TPD), axis=1, keepdims=True)
-    second = jnp.max(jnp.where(group, high, -1), axis=1, keepdims=True)
-    want_c = jnp.clip(jnp.where((at & 1) == 0, first, second), 0, TPD - 1)
-    want_r = to_row(want_c)
+    want_c = jnp.sum(jnp.where(sub == lane, want_r, 0), axis=1, keepdims=True)
     mine_c = jnp.zeros((TILE, 1), jnp.int32)
     for j in range(LIST):
         here = (wide == me * TPD + (at & 15)) & ((at >> 4) == j)
         mine_c = mine_c + jnp.sum(jnp.where(here, rows[j], 0), axis=1, keepdims=True)
-    mine_r = to_row(mine_c)
+    mine_r = diagonal(mine_c)
     own_c, own_r = mine_c >> 4, mine_r >> 4
     in_c, in_r = mine_c & 15, mine_r & 15
     real_c, real_r = at < ROWS, lane < ROWS
     lowest = jnp.min(jnp.where((own_c == own_r) & real_r, in_r, TPD), axis=1, keepdims=True)
     rank = jnp.where(in_c != lowest, 1, 0)
     slot_c = jnp.where(own_c == me, in_c, TPD + CAP * (relative(y, z, own_c) - 1) + rank)
-    slot_r = to_row(slot_c)
+    slot_r = diagonal(slot_c)
     local_c, local_r = (own_c == me) & real_c, (own_r == me) & real_r
     other_c, other_r = (own_c != me) & real_c, (own_r != me) & real_r
     l_perm, l_same = runs(slot_c, slot_r, local_c, local_r)
@@ -113,7 +123,6 @@
     found = {
         T_SLOT: slot_r,
         T_TILE: mine_r,
-        T_WANT: want_r,
         T_LPERM: l_perm,
         T_LSAME: l_same,
         T_LLAST: jnp.clip(count((slot_c <= lane) & local_c) - 1, 0, HALF - 1),
@@ -210,7 +219,7 @@
     o_stage, dq_stage, dk_stage, dv_stage = take(HPD), take(HPD), take(HPD), take(HPD)
     k_sum, v_sum = take(HPD), take(HPD)
     c_key, c_value, run_local, run_remote, run_back = take(5)
-    kv, seg, table, tab, t_sem = take(5)
+    kv, seg, table, want_table, tab, want_tab, t_sem = take(7)
     x_send, x_recv, c_send, c_recv, b_send, b_recv, y_send, y_recv = take(8)
 
     me, head = lax.axis_index("ctx"), lax.axis_index("head")
@@ -247,9 +256,9 @@
             ).start()
         pltpu.make_async_copy(src.at[:, pl.ds(*rows), columns(head, h)], dst.at[pair(head)], recv_sem).start()
 
-    def send_kv(s, h):
-        for n, rows in enumerate(PARTS_IN[s, h]):
-            send_in((k_in, v_in)[s], kv_loc[s, h][n], rows, h, x_send.at[2 + s], x_recv.at[2 + s, h, n])
+    def send_kv(s, h, n=0):
+        rows = PARTS_IN[s, h][n]
+        send_in((k_in, v_in)[s], kv_loc[s, h][n], rows, h, x_send.at[2 + s], x_recv.at[2 + s, h, n])
 
     def send_qg(h):
         send_in(q_in, q_loc[h], WHOLE[0], h, x_send.at[0], x_recv.at[0, h, 0])
@@ -285,46 +294,64 @@
                 device_id_type=MESH,
             ).start()
 
-    def forward_tiles(s, h):
+    def wait_kv(s, h, n=0):
+        wait_bytes(kv_loc[s, h][n], x_recv.at[2 + s, h, n])
+
+    def forward_tiles(s, h, n=0):
         stage, everything = (k_stage, v_stage)[s][h], (k_all, v_all)[s][h]
-        for n, rows in enumerate(PARTS_IN[s, h]):
-            local = kv_loc[s, h][n]
-            wait_bytes(local, x_recv.at[2 + s, h, n])
-
-            def pack(p, carry, local=local, rows=rows):
-                stage[p, pl.ds(*rows)] = local[tab[T_WANT, p]]
-                return carry
-
-            lax.fori_loop(0, NREM, pack, 0)
-            send_ctx(stage, everything, TPD, rows, rows, c_send.at[s, h, n], c_recv.at[s, h, n])
-
-            def keep(p, carry, local=local, rows=rows):
-                everything[p, pl.ds(*rows)] = local[p]
-                return carry
-
-            lax.fori_loop(0, TPD, keep, 0)
-
-    send_kv(0, 0)
+        rows, local = PARTS_IN[s, h][n], kv_loc[s, h][n]
+
+        def pack(p, carry):
+            stage[p, pl.ds(*rows)] = local[want_tab[0, p]]
+            return carry
+
+        lax.fori_loop(0, NREM, pack, 0)
+        send_ctx(stage, everything, TPD, rows, rows, c_send.at[s, h, n], c_recv.at[s, h, n])
+
+        def keep(p, carry):
+            everything[p, pl.ds(*rows)] = local[p]
+            return carry
+
+        lax.fori_loop(0, TPD, keep, 0)
+
+    def forward(s, h, n=0):
+        wait_kv(s, h, n)
+        forward_tiles(s, h, n)
+
+    send_kv(0, 0, 0)
+    fetches[0].wait()
+    want = diagonal(wanted_tiles(me, kv))
+    want_table[...] = jnp.broadcast_to(want, (8, TILE))
+    to_scalar = pltpu.make_async_copy(want_table, want_tab, t_sem.at[2])
+    to_scalar.start()
+    send_kv(0, 0, 1)
+    send_kv(0, 0, 2)
+    to_scalar.wait()
     send_kv(1, 0)
-    for fetch in fetches:
-        fetch.wait()
-    build_tables(me, kv, seg, table)
-    to_scalar = pltpu.make_async_copy(table, tab, t_sem.at[2])
+    forward(0, 0, 0)
+    send_kv(0, 1)
+    forward(0, 0, 1)
+    send_kv(1, 1)
+    forward(0, 0, 2)
+    send_kv(0, 2)
+    forward(1, 0)
+    send_kv(1, 2)
+    fetches[1].wait()
+    build_tables(me, kv, seg, want, table)
+    to_scalar = pltpu.make_async_copy(table, tab, t_sem.at[3])
     to_scalar.start()
+    forward(0, 1)
+    send_qg(0)
+    forward(1, 1)
+    send_qg(1)
+    forward(0, 2)
+    send_qg(2)
+    forward(1, 2)
     to_scalar.wait()
-    send_kv(0, 1)
-    forward_tiles(0, 0)
-    send_kv(1, 1)
-    send_qg(0)
-    forward_tiles(1, 0)
-    send_kv(0, 2)
-    send_kv(1, 2)
-    forward_tiles(0, 1)
-    send_qg(1)
-    forward_tiles(1, 1)
-    send_qg(2)
-    forward_tiles(0, 2)
-    forward_tiles(1, 2)
+
+    def send_back(s, h, n):
+        rows, stage, landing = PARTS_BACK[s, h][n], (k_stage, v_stage)[s][h], kv_back[s, h][n]
+        send_ctx(stage, landing, 0, rows, (0, rows[1]), b_send.at[s, h, n], b_recv.at[s, h, n])
 
     for h in range(HPD):
         wait_bytes(q_loc[h], x_recv.at[0, h, 0])
@@ -346,9 +373,9 @@
                 return carry
 
             lax.fori_loop(0, NREM, fill, 0)
-            for n, rows in enumerate(PARTS_BACK[s, h]):
-                landing = kv_back[s, h][n]
-                send_ctx(stage, landing, 0, rows, (0, rows[1]), b_send.at[s, h, n], b_recv.at[s, h, n])
+            for n in range(len(PARTS_BACK[s, h])):
+                if (s, h, n) not in sum(LATE.values(), ()):
+                    send_back(s, h, n)
         for s in range(2):
             sums = (k_sum, v_sum)[s][h]
             run_sums(tab, T_LPERM, T_LSAME, HALF, (c_key, c_value)[s], run_local)
@@ -366,6 +393,8 @@
             for n, rows in enumerate(PARTS_BACK[s, h]):
                 back = kv_back[s, h][n]
                 wait_bytes(back, b_recv.at[s, h, n])
+                for later in LATE.get((s, h, n), ()):
+                    send_back(*later)
                 run_sums(tab, T_BPERM, T_BSAME, NREM, back, run_back, shift=1, rows=rows[1])
 
                 def finish(p, carry, sums=sums, stage=stage, rows=rows):
@@ -388,17 +417,13 @@
 
 
 def hand_over(*refs):
-    source, result, (held, come, go) = refs[:4], refs[4:8], refs[8:]
-    pieces = [(a, p) for a in range(4) for p in range(2)]
-    coming = [pltpu.make_async_copy(source[a].at[p], held.at[a, p], come.at[a, p]) for a, p in pieces]
-    going = [pltpu.make_async_copy(held.at[a, p], result[a].at[p], go.at[a, p]) for a, p in pieces]
-    for copy in coming:
+    copies = [
+        pltpu.make_async_copy(refs[a].at[p], refs[4 + a].at[p], refs[8].at[a, p]) for a in range(4) for p in range(2)
+    ]
+    for copy in copies:
         copy.start()
-    for copy, onward in zip(coming, going):
+    for copy in copies:
         copy.wait()
-        onward.start()
-    for onward in going:
-        onward.wait()
 
 
 def body(query, key_in, value, out_grad, segment, kv_list):
@@ -425,8 +450,10 @@
             pltpu.VMEM((LIST, NCTX * TPD), jnp.int32),
             pltpu.VMEM((NCTX * TPD, TILE), jnp.int32),
             pltpu.VMEM((T_ROWS, TILE), jnp.int32),
+            pltpu.VMEM((8, TILE), jnp.int32),
             pltpu.SMEM((T_ROWS, TILE), jnp.int32),
-            pltpu.SemaphoreType.DMA((3,)),
+            pltpu.SMEM((8, TILE), jnp.int32),
+            pltpu.SemaphoreType.DMA((4,)),
             pltpu.SemaphoreType.DMA((4,)),
             pltpu.SemaphoreType.DMA((4, HPD, MOST_PARTS)),
             pltpu.SemaphoreType.DMA((2, HPD, MOST_PARTS)),
@@ -439,12 +466,12 @@
     )
     outs = pl.pallas_call(
         kernel,
-        out_shape=[jax.ShapeDtypeStruct(shape, bf16)] * 4,
+        out_shape=[pltpu.VMEM(shape, bf16)] * 4,
         in_specs=[pl.BlockSpec(memory_space=pl.ANY)] * 6,
         out_specs=[pl.BlockSpec(memory_space=pl.ANY)] * 4,
         scratch_shapes=scratch,
         compiler_params=pltpu.CompilerParams(
-            collective_id=0, has_side_effects=True, vmem_limit_bytes=60 * 1024 * 1024
+            collective_id=0, has_side_effects=True, vmem_limit_bytes=52 * 1024 * 1024
         ),
         cost_estimate=pl.CostEstimate(flops=7_250_000_000, bytes_accessed=12_600_000, transcendentals=4_718_592),
         name="sparse_attention",
@@ -454,12 +481,8 @@
         out_shape=[jax.ShapeDtypeStruct(shape, bf16)] * 4,
         in_specs=[pl.BlockSpec(memory_space=pl.ANY)] * 4,
         out_specs=[pl.BlockSpec(memory_space=pl.ANY)] * 4,
-        scratch_shapes=[
-            pltpu.VMEM((4,) + shape, bf16),
-            pltpu.SemaphoreType.DMA((4, 2)),
-            pltpu.SemaphoreType.DMA((4, 2)),
-        ],
-        compiler_params=pltpu.CompilerParams(vmem_limit_bytes=60 * 1024 * 1024),
+        scratch_shapes=[pltpu.SemaphoreType.DMA((4, 2))],
+        compiler_params=pltpu.CompilerParams(vmem_limit_bytes=4 * 1024 * 1024),
         name="hand_over",
     )(*outs)
     return tuple(o.reshape(tokens, width) for o in outs)

time: 173 us -> 168 us (0.971)
  Pallas kernels: 170 us -> 165 us
    pallas_call x1, Pallas kernels: 5.51 us -> 2.74 us  [body(): pl.pallas_call(hand_over, out_shape=[jax.ShapeDtypeStruct(shape, bf16)] *...]
    pallas_call x1, Pallas kernels: 165 us -> 163 us  [body(): pl.pallas_call(kernel, out_shape=[pltpu.VMEM(shape, bf16)] * 4, in_specs=...]
where the time goes in v3:
time: 168 us; the launch traced here: 166 us
  Pallas kernels  165 us (98%)
    pallas_call x1, Pallas kernels, body(): pl.pallas_call(kernel, out_shape=[pltpu.VMEM(shape, bf16)] * 4, in_specs=...  163 us

profile of v3, /device:TPU:25, one launch (start us, length us, event | category | flops | bytes accessed | tf_op | source)
XLA Modules:
  0.0 166.1 jit_solution(786830628474481724)
XLA Ops:
  0.6 162.7 %sparse_attention.1 = (bf16[2,128,3072]{2,1,0:T(8,128)(2,1)S(1)}, bf16[2,128,3072]{2,1,0:T(8,128)(2,1)S(1)}, bf16[2,128,3072]{2,1,0:T(8,128)(2,1)S(1)}, bf16[2,128,3072]{2,1,0:T(8,128)(2,1)S(1)}) custom-call(bf16[2,128,3072]{2,1,0:T(8,128)(2,1)} %bitcast.10, bf16[2,128,3072]{2,1,0:T(8,128)(2,1)} %bitcast.11, bf16[2,128,3072]{2,1,0:T(8,128)(2,1)} %bitcast.12, ...), custom_call_target="tpu_custom_call" | custom-call | flops 7249999872 | bytes 12600000 | tf_op jit(solution)/shard_map/sparse_attention/pallas_call | solution.py:467
  163.3 2.7 %hand_over.1 = (bf16[2,128,3072]{2,1,0:T(8,128)(2,1)}, bf16[2,128,3072]{2,1,0:T(8,128)(2,1)}, bf16[2,128,3072]{2,1,0:T(8,128)(2,1)}, bf16[2,128,3072]{2,1,0:T(8,128)(2,1)}) custom-call(bf16[2,128,3072]{2,1,0:T(8,128)(2,1)S(1)} %get-tuple-element.12.refs_0_, bf16[2,128,3072]{2,1,0:T(8,128)(2,1)S(1)} %get-tuple-element.13.refs_1_, ...), custom_call_target="tpu_custom_call" | custom-call | tf_op jit(solution)/shard_map/hand_over/pallas_call | solution.py:479

commit v4 on v3

--- a/solution.py
+++ b/solution.py
@@ -23,9 +23,10 @@
 MESH = pl.DeviceIdType.MESH
 
 OFFSETS = (
-    (0, 1), (2, 3), (0, 3), (2, 1), (1, 0), (3, 2), (3, 0), (1, 2),
-    (0, 2), (2, 0), (2, 2), (1, 1), (3, 3), (1, 3), (3, 1),
+    (1, 1), (3, 3), (1, 3), (3, 1), (0, 2), (2, 0), (2, 2), (1, 2), (3, 0), (3, 2), (1, 0), (2, 1), (0, 3), (2, 3), (0, 1),
 )
+
+AROUND = ((2, 0), (1, 0), (3, 0), (2, 1), (3, 1), (1, 1), (0, 1))
 
 WHOLE = ((0, TILE),)
 RISING = ((0, 32), (32, 32), (64, 64))
@@ -223,7 +224,7 @@
     x_send, x_recv, c_send, c_recv, b_send, b_recv, y_send, y_recv = take(8)
 
     me, head = lax.axis_index("ctx"), lax.axis_index("head")
-    y, z = me // 4, me % 4
+    y, z, core = me // 4, me % 4, head % 2
 
     fetches = [pltpu.make_async_copy(kv_in, kv, t_sem.at[0]), pltpu.make_async_copy(seg_in, seg, t_sem.at[1])]
     for fetch in fetches:
@@ -237,6 +238,10 @@
         pl.semaphore_signal(barrier, inc=1, device_id=(peer, head), device_id_type=MESH)
     pl.semaphore_wait(barrier, NHEAD - 1 + NCTX - 1)
 
+    def neighbour(chips, cores):
+        along = jnp.where(core == 0, chips, (4 - chips) % 4)
+        return ((head // 2 + along) % 4) * 2 + (core + cores) % 2
+
     def columns(owner, h):
         return pl.ds(pl.multiple_of((owner * HPD + h) * HEAD_DIM, HEAD_DIM), HEAD_DIM)
 
@@ -244,8 +249,8 @@
         return pl.ds(2 * index, 2)
 
     def send_in(src, dst, rows, h, send_sem, recv_sem):
-        for d in range(1, NHEAD):
-            peer = (head + d) % NHEAD
+        for chips, cores in AROUND:
+            peer = neighbour(chips, cores)
             pltpu.make_async_remote_copy(
                 src_ref=src.at[:, pl.ds(*rows), columns(peer, h)],
                 dst_ref=dst.at[pair(head)],
@@ -266,8 +271,8 @@
 
     def send_out(a, h, rows):
         src, dst = (o_stage, dq_stage, dk_stage, dv_stage)[a][h], (o_out, dq_out, dk_out, dv_out)[a]
-        for d in range(1, NHEAD):
-            peer = (head + d) % NHEAD
+        for chips, cores in AROUND:
+            peer = neighbour(chips, cores)
             pltpu.make_async_remote_copy(
                 src_ref=src.at[pair(peer), pl.ds(*rows)],
                 dst_ref=dst.at[:, pl.ds(*rows), columns(head, h)],
@@ -281,9 +286,10 @@
         ).start()
 
     def send_ctx(stage, landing, base, rows, landing_rows, send_sem, recv_sem):
-        for dy, dz in OFFSETS:
+        for one, two in OFFSETS:
+            dy, dz = jnp.where(core == 0, one, two), jnp.where(core == 0, two, one)
             there = dy * 4 + dz - 1
-            here = ((-dy) % 4) * 4 + (-dz) % 4 - 1
+            here = ((4 - dy) % 4) * 4 + (4 - dz) % 4 - 1
             peer = ((y + dy) % 4) * 4 + (z + dz) % 4
             pltpu.make_async_remote_copy(
                 src_ref=stage.at[pl.ds(CAP * there, CAP), pl.ds(*rows)],

time: 168 us -> 167 us (level)
  no operation moved by 1% of the time
where the time goes in v4:
time: 167 us; the launch traced here: 166 us
  Pallas kernels  165 us (99%)
    pallas_call x1, Pallas kernels, body(): pl.pallas_call(kernel, out_shape=[pltpu.VMEM(shape, bf16)] * 4, in_specs=...  162 us

profile of v4, /device:TPU:25, one launch (start us, length us, event | category | flops | bytes accessed | tf_op | source)
XLA Modules:
  0.0 165.7 jit_solution(2160091896958476746)
XLA Ops:
  0.6 162.4 %sparse_attention.1 = (bf16[2,128,3072]{2,1,0:T(8,128)(2,1)S(1)}, bf16[2,128,3072]{2,1,0:T(8,128)(2,1)S(1)}, bf16[2,128,3072]{2,1,0:T(8,128)(2,1)S(1)}, bf16[2,128,3072]{2,1,0:T(8,128)(2,1)S(1)}) custom-call(bf16[2,128,3072]{2,1,0:T(8,128)(2,1)} %bitcast.10, bf16[2,128,3072]{2,1,0:T(8,128)(2,1)} %bitcast.11, bf16[2,128,3072]{2,1,0:T(8,128)(2,1)} %bitcast.12, ...), custom_call_target="tpu_custom_call" | custom-call | flops 7249999872 | bytes 12600000 | tf_op jit(solution)/shard_map/sparse_attention/pallas_call | solution.py:473
  163.0 2.7 %hand_over.1 = (bf16[2,128,3072]{2,1,0:T(8,128)(2,1)}, bf16[2,128,3072]{2,1,0:T(8,128)(2,1)}, bf16[2,128,3072]{2,1,0:T(8,128)(2,1)}, bf16[2,128,3072]{2,1,0:T(8,128)(2,1)}) custom-call(bf16[2,128,3072]{2,1,0:T(8,128)(2,1)S(1)} %get-tuple-element.12.refs_0_, bf16[2,128,3072]{2,1,0:T(8,128)(2,1)S(1)} %get-tuple-element.13.refs_1_, ...), custom_call_target="tpu_custom_call" | custom-call | tf_op jit(solution)/shard_map/hand_over/pallas_call | solution.py:485

commit v5 on v4

--- a/solution.py
+++ b/solution.py
@@ -29,12 +29,13 @@
 AROUND = ((2, 0), (1, 0), (3, 0), (2, 1), (3, 1), (1, 1), (0, 1))
 
 WHOLE = ((0, TILE),)
+HALVES = ((0, 64), (64, 64))
 RISING = ((0, 32), (32, 32), (64, 64))
 FALLING = ((0, 64), (64, 32), (96, 32))
 PARTS_IN = {(s, h): WHOLE for s in range(2) for h in range(HPD)} | {(0, 0): RISING}
-PARTS_BACK = {(s, h): WHOLE for s in range(2) for h in range(HPD)} | {(1, HPD - 1): FALLING}
+PARTS_BACK = {(s, h): HALVES for s in range(2) for h in range(HPD)} | {(0, HPD - 1): HALVES, (1, HPD - 1): FALLING}
 MOST_PARTS = 3
-LATE = {(1, 1, 0): ((1, 2, 0),), (0, 2, 0): ((1, 2, 1), (1, 2, 2))}
+LATE = {(1, 1, 1): ((1, 2, 0),), (0, 2, 0): ((1, 2, 1), (1, 2, 2))}
 
 T_SLOT, T_TILE = 0, 1
 T_LPERM, T_LSAME, T_LLAST = 3, 4, 5

time: 167 us -> 164 us (0.982)
  Pallas kernels: 165 us -> 161 us
    pallas_call x1, Pallas kernels: 162 us -> 159 us  [body(): pl.pallas_call(kernel, out_shape=[pltpu.VMEM(shape, bf16)] * 4, in_specs=...]
where the time goes in v5:
time: 164 us; the launch traced here: 162 us
  Pallas kernels  161 us (98%)
    pallas_call x1, Pallas kernels, body(): pl.pallas_call(kernel, out_shape=[pltpu.VMEM(shape, bf16)] * 4, in_specs=...  159 us

profile of v5, /device:TPU:25, one launch (start us, length us, event | category | flops | bytes accessed | tf_op | source)
XLA Modules:
  0.0 162.0 jit_solution(11480475429701390434)
XLA Ops:
  0.6 158.6 %sparse_attention.1 = (bf16[2,128,3072]{2,1,0:T(8,128)(2,1)S(1)}, bf16[2,128,3072]{2,1,0:T(8,128)(2,1)S(1)}, bf16[2,128,3072]{2,1,0:T(8,128)(2,1)S(1)}, bf16[2,128,3072]{2,1,0:T(8,128)(2,1)S(1)}) custom-call(bf16[2,128,3072]{2,1,0:T(8,128)(2,1)} %bitcast.10, bf16[2,128,3072]{2,1,0:T(8,128)(2,1)} %bitcast.11, bf16[2,128,3072]{2,1,0:T(8,128)(2,1)} %bitcast.12, ...), custom_call_target="tpu_custom_call" | custom-call | flops 7249999872 | bytes 12600000 | tf_op jit(solution)/shard_map/sparse_attention/pallas_call | solution.py:474
  159.2 2.7 %hand_over.1 = (bf16[2,128,3072]{2,1,0:T(8,128)(2,1)}, bf16[2,128,3072]{2,1,0:T(8,128)(2,1)}, bf16[2,128,3072]{2,1,0:T(8,128)(2,1)}, bf16[2,128,3072]{2,1,0:T(8,128)(2,1)}) custom-call(bf16[2,128,3072]{2,1,0:T(8,128)(2,1)S(1)} %get-tuple-element.12.refs_0_, bf16[2,128,3072]{2,1,0:T(8,128)(2,1)S(1)} %get-tuple-element.13.refs_1_, ...), custom_call_target="tpu_custom_call" | custom-call | tf_op jit(solution)/shard_map/hand_over/pallas_call | solution.py:486

commit v6 on v5

--- a/solution.py
+++ b/solution.py
@@ -333,26 +333,26 @@
     to_scalar.start()
     send_kv(0, 0, 1)
     send_kv(0, 0, 2)
+    send_kv(1, 0)
+    send_kv(0, 1)
     to_scalar.wait()
-    send_kv(1, 0)
     forward(0, 0, 0)
-    send_kv(0, 1)
+    send_kv(1, 1)
+    send_kv(0, 2)
     forward(0, 0, 1)
-    send_kv(1, 1)
+    send_kv(1, 2)
+    send_qg(0)
     forward(0, 0, 2)
-    send_kv(0, 2)
+    send_qg(1)
+    send_qg(2)
     forward(1, 0)
-    send_kv(1, 2)
     fetches[1].wait()
     build_tables(me, kv, seg, want, table)
     to_scalar = pltpu.make_async_copy(table, tab, t_sem.at[3])
     to_scalar.start()
     forward(0, 1)
-    send_qg(0)
     forward(1, 1)
-    send_qg(1)
     forward(0, 2)
-    send_qg(2)
     forward(1, 2)
     to_scalar.wait()
 

time: 164 us -> 164 us (level)
  no operation moved by 1% of the time
where the time goes in v6:
time: 164 us; the launch traced here: 162 us
  Pallas kernels  161 us (98%)
    pallas_call x1, Pallas kernels, body(): pl.pallas_call(kernel, out_shape=[pltpu.VMEM(shape, bf16)] * 4, in_specs=...  159 us

profile of v6, /device:TPU:25, one launch (start us, length us, event | category | flops | bytes accessed | tf_op | source)
XLA Modules:
  0.0 162.0 jit_solution(15281920164936390881)
XLA Ops:
  0.6 158.6 %sparse_attention.1 = (bf16[2,128,3072]{2,1,0:T(8,128)(2,1)S(1)}, bf16[2,128,3072]{2,1,0:T(8,128)(2,1)S(1)}, bf16[2,128,3072]{2,1,0:T(8,128)(2,1)S(1)}, bf16[2,128,3072]{2,1,0:T(8,128)(2,1)S(1)}) custom-call(bf16[2,128,3072]{2,1,0:T(8,128)(2,1)} %bitcast.10, bf16[2,128,3072]{2,1,0:T(8,128)(2,1)} %bitcast.11, bf16[2,128,3072]{2,1,0:T(8,128)(2,1)} %bitcast.12, ...), custom_call_target="tpu_custom_call" | custom-call | flops 7249999872 | bytes 12600000 | tf_op jit(solution)/shard_map/sparse_attention/pallas_call | solution.py:474
  159.2 2.7 %hand_over.1 = (bf16[2,128,3072]{2,1,0:T(8,128)(2,1)}, bf16[2,128,3072]{2,1,0:T(8,128)(2,1)}, bf16[2,128,3072]{2,1,0:T(8,128)(2,1)}, bf16[2,128,3072]{2,1,0:T(8,128)(2,1)}) custom-call(bf16[2,128,3072]{2,1,0:T(8,128)(2,1)S(1)} %get-tuple-element.12.refs_0_, bf16[2,128,3072]{2,1,0:T(8,128)(2,1)S(1)} %get-tuple-element.13.refs_1_, ...), custom_call_target="tpu_custom_call" | custom-call | tf_op jit(solution)/shard_map/hand_over/pallas_call | solution.py:486
